TPU v7x, 128 devices: a whole 4x4x4 slice. The times are simulated.
128 devices in a mesh: dp: 16 (over y, z_hi, core), tensor: 8 (over x, z_lo).
Axes of the slice: x: 4, y: 4, z: 4 (z_hi: 2, z_lo: 2; z = z_hi * 2 + z_lo), core: 2. Of those that a mesh axis runs over, the one named last changes fastest.
Arguments:
- tokens: bfloat16 [16384, 2048], P(('dp', 'tensor')), may hold values from -6 to 6
- starts: int32 [16], P('dp'), may hold values from 0 to 768, as said below
- w_query: bfloat16 [2048, 2048], P('dp', 'tensor'), may hold values from -0.125 to 0.125
- w_key: bfloat16 [2048, 2048], P('dp', 'tensor'), may hold values from -0.125 to 0.125
- w_value: bfloat16 [2048, 2048], P('dp', 'tensor'), may hold values from -0.125 to 0.125
- w_out: bfloat16 [2048, 2048], P('tensor', 'dp'), may hold values from -2 to 2
- w_gate: bfloat16 [2048, 5504], P('dp', 'tensor'), may hold values from -0.125 to 0.125
- w_up: bfloat16 [2048, 5504], P('dp', 'tensor'), may hold values from -0.125 to 0.125
- w_down: bfloat16 [5504, 2048], P('tensor', 'dp'), may hold values from -0.078125 to 0.078125
- gain_attn: float32 [2048], P(('dp', 'tensor')), may hold values from 0.5 to 1.5
- gain_mlp: float32 [2048], P(('dp', 'tensor')), may hold values from 0.5 to 1.5
- cotangent: bfloat16 [16384, 2048], P(('dp', 'tensor')), may hold values from -6 to 6
Outputs:
- output: bfloat16 [16384, 2048], P(('dp', 'tensor'))
- grad_tokens: bfloat16 [16384, 2048], P(('dp', 'tensor'))
- grad_query: float32 [2048, 2048], P('dp', 'tensor')
- grad_key: float32 [2048, 2048], P('dp', 'tensor')
- grad_value: float32 [2048, 2048], P('dp', 'tensor')
- grad_out: float32 [2048, 2048], P('tensor', 'dp')
- grad_gate: float32 [2048, 5504], P('dp', 'tensor')
- grad_up: float32 [2048, 5504], P('dp', 'tensor')
- grad_down: float32 [5504, 2048], P('tensor', 'dp')
- grad_gain_attn: float32 [2048], P(('dp', 'tensor'))
- grad_gain_mlp: float32 [2048], P(('dp', 'tensor'))
Inputs may be any that keep to these rules, and one draw needn't show every extreme that they name: `starts`: the start of the one picture piece of each sequence; its 256 positions attend to each other both ways.
All inputs are finite; a program needn't handle non-finite values.
Results may differ from a plain program's by a relative error of at most 0.03.
Values may be sent and summed in bfloat16 or wider, within the bound.
A program may use at most 128 MiB of HBM per device.

v0:
```python
import math

import jax
import jax.numpy as jnp
from jax import lax
from jax.sharding import PartitionSpec as P

HD = 128
BLOCK = 512
PIECE = 256


EPS = 1e-05
NEG = -1e30


def dot_plain(left, right):
    return jnp.dot(left, right, preferred_element_type=jnp.float32)


def dot_rows(left, right):
    return lax.dot_general(
        left, right, (((0,), (0,)), ((), ())), preferred_element_type=jnp.float32
    )


def dot_cols(left, right):
    return lax.dot_general(
        left, right, (((1,), (1,)), ((), ())), preferred_element_type=jnp.float32
    )


def rope_parts(length):
    half = HD // 2
    index = jnp.arange(half).astype(jnp.float32)
    freq = jnp.exp(index * (-2.0 * math.log(10000.0) / HD))
    angle = jnp.arange(length).astype(jnp.float32)[:, None] * freq[None, :]
    return (jnp.cos(angle)[:, None, :], jnp.sin(angle)[:, None, :])


def rotate(field, cosine, sine):
    half = HD // 2
    first = field[..., :half]
    second = field[..., half:]
    return jnp.concatenate(
        [first * cosine - second * sine, second * cosine + first * sine], axis=-1
    )


def unrotate(field, cosine, sine):
    half = HD // 2
    first = field[..., :half]
    second = field[..., half:]
    return jnp.concatenate(
        [first * cosine + second * sine, second * cosine - first * sine], axis=-1
    )


def norm_rows(value_rows, gain):
    row_scales = lax.rsqrt(jnp.mean(value_rows * value_rows, axis=-1, keepdims=True) + EPS)
    return ((value_rows * row_scales * gain).astype(jnp.bfloat16), row_scales)


def norm_back(incoming_gradient, value_rows, row_scales, gain):
    normalized_input = value_rows * row_scales
    gain_gradient = jnp.sum(incoming_gradient * normalized_input, axis=0)
    rescaled_rows = incoming_gradient * gain
    inner_product = jnp.mean(rescaled_rows * normalized_input, axis=-1, keepdims=True)
    return (gain_gradient, row_scales * (rescaled_rows - normalized_input * inner_product))


def spread_rows(piece):
    return lax.all_gather(piece, "tensor", axis=0, tiled=True)


def sum_rows(partial_sum):
    return lax.psum_scatter(
        partial_sum.astype(jnp.bfloat16), "tensor", scatter_dimension=0, tiled=True
    ).astype(jnp.float32)


def fetch_attention(w_query, w_key, w_value, w_out):
    return (
        lax.all_gather(w_query, "dp", axis=0, tiled=True),
        lax.all_gather(w_key, "dp", axis=0, tiled=True),
        lax.all_gather(w_value, "dp", axis=0, tiled=True),
        lax.all_gather(w_out, "dp", axis=1, tiled=True),
    )


def fetch_mlp(w_gate, w_up, w_down):
    return (
        lax.all_gather(w_gate, "dp", axis=0, tiled=True),
        lax.all_gather(w_up, "dp", axis=0, tiled=True),
        lax.all_gather(w_down, "dp", axis=1, tiled=True),
    )


def on_device(
    tokens,
    starts,
    w_query,
    w_key,
    w_value,
    w_out,
    w_gate,
    w_up,
    w_down,
    gain_attn,
    gain_mlp,
    cotangent,
):
    gain_one, gain_two = (
        lax.all_gather(gain_attn, ("dp", "tensor"), axis=0, tiled=True),
        lax.all_gather(gain_mlp, ("dp", "tensor"), axis=0, tiled=True),
    )
    start = starts[0]
    xf = tokens.astype(jnp.float32)
    full_q, full_k, full_v, full_o = fetch_attention(w_query, w_key, w_value, w_out)
    h_one, r_one = norm_rows(xf, gain_one)
    h_one_full = spread_rows(h_one)
    length = h_one_full.shape[0]
    heads = full_q.shape[1] // HD
    cosine, sine = rope_parts(length)
    query = rotate(dot_plain(h_one_full, full_q).reshape(length, heads, HD), cosine, sine).astype(
        jnp.bfloat16
    )
    keys = rotate(dot_plain(h_one_full, full_k).reshape(length, heads, HD), cosine, sine).astype(
        jnp.bfloat16
    )
    value_rows = dot_plain(h_one_full, full_v).astype(jnp.bfloat16).reshape(length, heads, HD)
    count = length // BLOCK
    scale = HD ** (-0.5)
    positions = jnp.arange(length, dtype=jnp.int32)
    inside_all = (positions >= start) & (positions < start + PIECE)

    def block_scores(first):
        rows = first + jnp.arange(BLOCK, dtype=jnp.int32)
        inside_rows = (rows >= start) & (rows < start + PIECE)
        allowed = (positions[None, :] <= rows[:, None]) | inside_rows[:, None] & inside_all[None, :]
        q_block = lax.dynamic_slice_in_dim(query, first, BLOCK, 0)
        scores = (
            jnp.einsum("qhd,khd->hqk", q_block, keys, preferred_element_type=jnp.float32) * scale
        )
        return (jnp.where(allowed[None], scores, NEG), q_block)

    def forward_block(index):
        scores, q_block = block_scores(index * BLOCK)
        top = jnp.max(scores, axis=-1, keepdims=True)
        expo = jnp.exp(scores - top)
        total = jnp.sum(expo, axis=-1, keepdims=True)
        probs = (expo / total).astype(jnp.bfloat16)
        block_out = jnp.einsum(
            "hqk,khd->qhd", probs, value_rows, preferred_element_type=jnp.float32
        )
        return (block_out.astype(jnp.bfloat16), (top + jnp.log(total))[..., 0])

    out_blocks, lse = lax.map(forward_block, jnp.arange(count))
    heads_out = out_blocks.reshape(length, heads * HD)
    y_one = xf + sum_rows(dot_plain(heads_out, full_o))
    full_g, full_u, full_d = fetch_mlp(w_gate, w_up, w_down)
    h_two, r_two = norm_rows(y_one, gain_two)
    h_two_full = spread_rows(h_two)
    gate = dot_plain(h_two_full, full_g)
    up = dot_plain(h_two_full, full_u)
    sigma = jax.nn.sigmoid(gate)
    act = (gate * sigma * up).astype(jnp.bfloat16)
    output = (y_one + sum_rows(dot_plain(act, full_d))).astype(jnp.bfloat16)
    full_g, full_u, full_d = fetch_mlp(w_gate, w_up, w_down)
    d_out = cotangent.astype(jnp.float32)
    d_mlp = spread_rows(cotangent)
    grad_down = dot_rows(act, d_mlp)
    d_act = dot_cols(d_mlp, full_d)
    d_gate = (d_act * up * sigma * (1.0 + gate * (1.0 - sigma))).astype(jnp.bfloat16)
    d_up = (d_act * gate * sigma).astype(jnp.bfloat16)
    grad_gate = dot_rows(h_two_full, d_gate)
    grad_up = dot_rows(h_two_full, d_up)
    d_h_two = sum_rows(dot_cols(d_gate, full_g) + dot_cols(d_up, full_u))
    grad_gain_two, d_norm_two = norm_back(d_h_two, y_one, r_two, gain_two)
    d_y_one = d_out + d_norm_two
    grad_gate, grad_up, grad_down = (
        lax.psum_scatter(
            grad_gate.astype(jnp.bfloat16), "dp", scatter_dimension=0, tiled=True
        ).astype(jnp.float32),
        lax.psum_scatter(
            grad_up.astype(jnp.bfloat16), "dp", scatter_dimension=0, tiled=True
        ).astype(jnp.float32),
        lax.psum_scatter(
            grad_down.astype(jnp.bfloat16), "dp", scatter_dimension=1, tiled=True
        ).astype(jnp.float32),
    )
    full_q, full_k, full_v, full_o = fetch_attention(w_query, w_key, w_value, w_out)
    d_attn = spread_rows(d_y_one.astype(jnp.bfloat16))
    grad_out = dot_rows(heads_out, d_attn)
    d_heads = dot_cols(d_attn, full_o).astype(jnp.bfloat16).reshape(length, heads, HD)

    def backward_block(carry, index):
        first = index * BLOCK
        scores, q_block = block_scores(first)
        lse_block = lax.dynamic_index_in_dim(lse, index, 0, keepdims=False)
        probs = jnp.exp(scores - lse_block[..., None])
        probs_low = probs.astype(jnp.bfloat16)
        d_block = lax.dynamic_slice_in_dim(d_heads, first, BLOCK, 0)
        d_probs = jnp.einsum(
            "qhd,khd->hqk", d_block, value_rows, preferred_element_type=jnp.float32
        )
        delta = jnp.sum(probs * d_probs, axis=-1, keepdims=True)
        d_scores = (probs * (d_probs - delta) * scale).astype(jnp.bfloat16)
        d_q_block = jnp.einsum("hqk,khd->qhd", d_scores, keys, preferred_element_type=jnp.float32)
        d_k_sum = carry[0] + jnp.einsum(
            "hqk,qhd->khd", d_scores, q_block, preferred_element_type=jnp.float32
        )
        d_v_sum = carry[1] + jnp.einsum(
            "hqk,qhd->khd", probs_low, d_block, preferred_element_type=jnp.float32
        )
        return ((d_k_sum, d_v_sum), d_q_block)

    zero_heads = jnp.zeros((length, heads, HD), jnp.float32)
    (d_keys, d_values), d_query = lax.scan(
        backward_block, (zero_heads, zero_heads), jnp.arange(count)
    )
    d_query = d_query.reshape(length, heads, HD)
    d_raw_q = unrotate(d_query, cosine, sine).astype(jnp.bfloat16).reshape(length, heads * HD)
    d_raw_k = unrotate(d_keys, cosine, sine).astype(jnp.bfloat16).reshape(length, heads * HD)
    d_raw_v = d_values.astype(jnp.bfloat16).reshape(length, heads * HD)
    grad_query = dot_rows(h_one_full, d_raw_q)
    grad_key = dot_rows(h_one_full, d_raw_k)
    grad_value = dot_rows(h_one_full, d_raw_v)
    d_h_one = sum_rows(
        dot_cols(d_raw_q, full_q) + dot_cols(d_raw_k, full_k) + dot_cols(d_raw_v, full_v)
    )
    grad_gain_one, d_norm_one = norm_back(d_h_one, xf, r_one, gain_one)
    grad_tokens = (d_y_one + d_norm_one).astype(jnp.bfloat16)
    grad_query, grad_key, grad_value, grad_out = (
        lax.psum_scatter(
            grad_query.astype(jnp.bfloat16), "dp", scatter_dimension=0, tiled=True
        ).astype(jnp.float32),
        lax.psum_scatter(
            grad_key.astype(jnp.bfloat16), "dp", scatter_dimension=0, tiled=True
        ).astype(jnp.float32),
        lax.psum_scatter(
            grad_value.astype(jnp.bfloat16), "dp", scatter_dimension=0, tiled=True
        ).astype(jnp.float32),
        lax.psum_scatter(
            grad_out.astype(jnp.bfloat16), "dp", scatter_dimension=1, tiled=True
        ).astype(jnp.float32),
    )
    grad_gain_attn, grad_gain_mlp = (
        lax.psum_scatter(grad_gain_one, ("dp", "tensor"), scatter_dimension=0, tiled=True),
        lax.psum_scatter(grad_gain_two, ("dp", "tensor"), scatter_dimension=0, tiled=True),
    )
    return (
        output,
        grad_tokens,
        grad_query,
        grad_key,
        grad_value,
        grad_out,
        grad_gate,
        grad_up,
        grad_down,
        grad_gain_attn,
        grad_gain_mlp,
    )


def solution(mesh):
    in_specs = (
        P(("dp", "tensor"), None),
        P("dp"),
        P("dp", "tensor"),
        P("dp", "tensor"),
        P("dp", "tensor"),
        P("tensor", "dp"),
        P("dp", "tensor"),
        P("dp", "tensor"),
        P("tensor", "dp"),
        P(("dp", "tensor")),
        P(("dp", "tensor")),
        P(("dp", "tensor"), None),
    )
    out_specs = (
        P(("dp", "tensor"), None),
        P(("dp", "tensor"), None),
        P("dp", "tensor"),
        P("dp", "tensor"),
        P("dp", "tensor"),
        P("tensor", "dp"),
        P("dp", "tensor"),
        P("dp", "tensor"),
        P("tensor", "dp"),
        P(("dp", "tensor")),
        P(("dp", "tensor")),
    )
    return jax.shard_map(
        on_device, mesh=mesh, in_specs=in_specs, out_specs=out_specs, check_vma=False
    )
```

profile of v0, /device:TPU:1, one launch (start us, length us, event | category | flops | bytes accessed | tf_op | source)
XLA Modules:
  0.0 1681.3 jit_solution(5794068113165426100)
XLA Ops:
  9.7 69.8 %all-reduce.5 = (f32[2048]{0:T(1024)S(1)}, f32[2048]{0:T(1024)S(1)}) all-reduce(f32[2048]{0:T(1024)S(1)} %dynamic-update-slice, f32[2048]{0:T(1024)S(1)} %dynamic-update-slice.1), channel_id=1, replica_groups=mesh['dp'=16,'tensor'=8] {'dp','tensor'}, use_global_device_ids=true, to_apply=%add | all-reduce | flops 4096 | bytes 32768
  80.8 2.0 fusion.81
  87.4 81.9 %all-gather.12.cloned.1.call-done = bf16[1024,2048]{1,0:T(8,128)(2,1)} async-done(((bf16[128,2048]{1,0:T(8,128)(2,1)}), bf16[1024,2048]{1,0:T(8,128)(2,1)}) %all-gather.12.cloned.1.call-update) | async-done | bytes 4194320 | tf_op jit(solution)/shard_map/all_gather | solution.py:73
  169.3 3.8 convolution_convert_fusion.10
  173.4 46.4 %all-gather.16.cloned.1.call-done = bf16[2048,256]{1,0:T(8,128)(2,1)} async-done(((bf16[128,256]{1,0:T(8,128)(2,1)}), bf16[2048,256]{1,0:T(8,128)(2,1)}) %all-gather.16.cloned.1.call-update) | async-done | bytes 1048592 | tf_op jit(solution)/shard_map/all_gather | solution.py:85
  219.8 3.8 fusion.94
  227.3 38.5 %all-gather.14.cloned.1.call-done = bf16[2048,256]{1,0:T(8,128)(2,1)} async-done(((bf16[128,256]{1,0:T(8,128)(2,1)}), bf16[2048,256]{1,0:T(8,128)(2,1)}) %all-gather.14.cloned.1.call-update) | async-done | bytes 1048592 | tf_op jit(solution)/shard_map/all_gather | solution.py:84
  265.8 3.8 fusion.93
  270.5 2.4 copy.91
  274.1 2.5 subtract_convert_fusion.2
  277.2 14.9 while.33
  292.1 19.9 %all-gather.20.cloned.1.call-done = bf16[256,2048]{1,0:T(8,128)(2,1)} async-done(((bf16[256,128]{1,0:T(8,128)(2,1)}), bf16[256,2048]{1,0:T(8,128)(2,1)}) %all-gather.20.cloned.1.call-update) | async-done | bytes 1048592 | tf_op jit(solution)/shard_map/all_gather | solution.py:87
  312.0 4.5 convolution_convert_fusion.1
  317.3 87.9 %reduce-scatter.20.cloned.1.call-done = bf16[128,2048]{1,0:T(8,128)(2,1)} async-done(((bf16[1024,2048]{1,0:T(8,128)(2,1)}), bf16[128,2048]{1,0:T(8,128)(2,1)}) %reduce-scatter.20.cloned.1.call-update) | async-done | bytes 524304 | tf_op jit(solution)/shard_map/reduce_scatter | solution.py:77
  406.5 2.0 multiply_convert_fusion.4
  410.7 51.0 %all-gather.26.cloned.1.call-done = bf16[2048,688]{0,1:T(8,128)(2,1)} async-done(((bf16[128,688]{0,1:T(8,128)(2,1)}), bf16[2048,688]{0,1:T(8,128)(2,1)}) %all-gather.26.cloned.1.call-update) | async-done | bytes 2818064 | tf_op jit(solution)/shard_map/all_gather | solution.py:94
  461.6 90.1 %all-gather.22.cloned.1.call-done = bf16[1024,2048]{1,0:T(8,128)(2,1)} async-done(((bf16[128,2048]{1,0:T(8,128)(2,1)}), bf16[1024,2048]{1,0:T(8,128)(2,1)}) %all-gather.22.cloned.1.call-update) | async-done | bytes 4194320 | tf_op jit(solution)/shard_map/all_gather | solution.py:73
  551.8 7.8 fusion.96
  559.5 50.3 %all-gather.24.cloned.1.call-done = bf16[2048,688]{0,1:T(8,128)(2,1)} async-done(((bf16[128,688]{0,1:T(8,128)(2,1)}), bf16[2048,688]{0,1:T(8,128)(2,1)}) %all-gather.24.cloned.1.call-update) | async-done | bytes 2818064 | tf_op jit(solution)/shard_map/all_gather | solution.py:93
  609.8 7.7 fusion.95
  617.5 45.8 %all-gather.28.cloned.1.call-done = bf16[688,2048]{1,0:T(8,128)(2,1)} async-done(((bf16[688,128]{1,0:T(8,128)(2,1)}), bf16[688,2048]{1,0:T(8,128)(2,1)}) %all-gather.28.cloned.1.call-update) | async-done | bytes 2818064 | tf_op jit(solution)/shard_map/all_gather | solution.py:95
  663.3 89.6 %all-gather.30.cloned.1.call-done = bf16[1024,2048]{1,0:T(8,128)(2,1)} async-done(((bf16[128,2048]{1,0:T(8,128)(2,1)}), bf16[1024,2048]{1,0:T(8,128)(2,1)}) %all-gather.30.cloned.1.call-update) | async-done | bytes 4194320 | tf_op jit(solution)/shard_map/all_gather | solution.py:73
  752.9 10.0 multiply_convert_fusion.1
  762.9 3.5 fusion.97
  766.5 13.8 add_convert_fusion.1
  780.4 93.0 %reduce-scatter.24.cloned.1.call-done = bf16[128,2048]{1,0:T(8,128)(2,1)} async-done(((bf16[1024,2048]{1,0:T(8,128)(2,1)}), bf16[128,2048]{1,0:T(8,128)(2,1)}) %reduce-scatter.24.cloned.1.call-update) | async-done | bytes 524304 | tf_op jit(solution)/shard_map/reduce_scatter | solution.py:77
  874.9 2.3 fusion.90
  877.3 7.2 convolution_convert_fusion.4
  884.5 4.7 copy.83
  889.3 7.2 convolution_convert_fusion.3
  896.5 4.6 copy.79
  901.2 7.3 convolution_convert_fusion.2
  908.4 4.6 copy.81
  913.1 55.0 %all-gather.32.cloned.1.call-done = bf16[1024,2048]{1,0:T(8,128)(2,1)} async-done(((bf16[128,2048]{1,0:T(8,128)(2,1)}), bf16[1024,2048]{1,0:T(8,128)(2,1)}) %all-gather.32.cloned.1.call-update) | async-done | bytes 4194320 | tf_op jit(solution)/shard_map/all_gather | solution.py:73
  968.1 4.4 convolution_convert_fusion.5
  972.5 2.3 copy.77
  975.1 3.8 convolution_convert_fusion.9
  978.9 58.2 %while.34 = (s32[]{:T(128)}, f32[1024,2,128]{0,2,1:T(8,128)}, f32[1024,2,128]{0,2,1:T(8,128)S(1)}, f32[2,512,2,128]{3,1,0,2:T(8,128)}, s32[2]{0:T(128)S(1)}, /*i...) while((s32[]{:T(128)}, f32[1024,2,128]{0,2,1:T(8,128)}, ...), condition=%wide.region_12.13_spmd.clone.clone.clone, body=%wide.region_10.12_spmd.clone.clone.clone.sunk | while | flops 1359488512 | bytes 71322960 | solution.py:219
  984.0 2.2 subtract_exponential_fusion.3
  986.2 2.0 copy-done
  988.8 2.7 fusion.187
  991.5 8.6 fusion.188
  1000.1 8.0 fusion.190
  1013.1 2.2 subtract_exponential_fusion.3
  1015.2 2.0 copy-done
  1017.8 2.7 fusion.187
  1020.6 8.6 fusion.188
  1029.1 8.0 fusion.190
  1037.2 4.8 convolution_convert_fusion.6
  1043.7 3.1 add_convert_fusion.2
  1047.3 4.6 convolution_convert_fusion.8
  1052.8 4.6 convolution_convert_fusion.7
  1060.2 3.4 add_convert_fusion
  1065.0 6.9 convolution_convert_fusion
  1073.9 52.7 %reduce-scatter.36.cloned.1.call-done = bf16[128,688]{1,0:T(8,128)(2,1)} async-done(((bf16[2048,688]{1,0:T(8,128)(2,1)}), bf16[128,688]{1,0:T(8,128)(2,1)}) %reduce-scatter.36.cloned.1.call-update) | async-done | bytes 176144
  1128.5 76.1 %reduce-scatter.38.cloned.1.call-done = bf16[128,688]{1,0:T(8,128)(2,1)} async-done(((bf16[2048,688]{1,0:T(8,128)(2,1)}), bf16[128,688]{1,0:T(8,128)(2,1)}) %reduce-scatter.38.cloned.1.call-update) | async-done | bytes 176144
  1206.4 66.7 %reduce-scatter.34.cloned.1.call-done = bf16[128,256]{1,0:T(8,128)(2,1)} async-done(((bf16[2048,256]{1,0:T(8,128)(2,1)}), bf16[128,256]{1,0:T(8,128)(2,1)}) %reduce-scatter.34.cloned.1.call-update) | async-done | bytes 65552
  1274.7 68.4 %reduce-scatter.32.cloned.1.call-done = bf16[128,256]{1,0:T(8,128)(2,1)} async-done(((bf16[2048,256]{1,0:T(8,128)(2,1)}), bf16[128,256]{1,0:T(8,128)(2,1)}) %reduce-scatter.32.cloned.1.call-update) | async-done | bytes 65552 | tf_op jit(solution)/shard_map/reduce_scatter | solution.py:241
  1344.6 68.1 %reduce-scatter.28.cloned.1.call-done = bf16[128,256]{1,0:T(8,128)(2,1)} async-done(((bf16[2048,256]{1,0:T(8,128)(2,1)}), bf16[128,256]{1,0:T(8,128)(2,1)}) %reduce-scatter.28.cloned.1.call-update) | async-done | bytes 65552 | tf_op jit(solution)/shard_map/reduce_scatter | solution.py:235
  1414.2 68.4 %reduce-scatter.30.cloned.1.call-done = bf16[128,256]{1,0:T(8,128)(2,1)} async-done(((bf16[2048,256]{1,0:T(8,128)(2,1)}), bf16[128,256]{1,0:T(8,128)(2,1)}) %reduce-scatter.30.cloned.1.call-update) | async-done | bytes 65552 | tf_op jit(solution)/shard_map/reduce_scatter | solution.py:238
  1484.2 92.2 %reduce-scatter.26.cloned.1.call-done = bf16[128,2048]{1,0:T(8,128)(2,1)} async-done(((bf16[1024,2048]{1,0:T(8,128)(2,1)}), bf16[128,2048]{1,0:T(8,128)(2,1)}) %reduce-scatter.26.cloned.1.call-update) | async-done | bytes 524304 | tf_op jit(solution)/shard_map/reduce_scatter | solution.py:77
  1577.8 80.3 %all-reduce.4 = (f32[2048]{0:T(1024)S(1)}, f32[2048]{0:T(1024)S(1)}) all-reduce(f32[2048]{0:T(1024)S(1)} %get-tuple-element.491, f32[2048]{0:T(1024)S(1)} %get-tuple-element.489), channel_id=13, replica_groups=mesh['dp'=16,'tensor'=8] {'dp','tensor'}, use_global_device_ids=true, to_apply=%region_23.24.clone | all-reduce | flops 4096 | bytes 32768
  1659.3 11.6 reduce-scatter.22.cloned.1.call-done
  1671.0 3.0 fusion.76
  (186 shorter events, 61.4 us)
Async XLA Ops:
  7.2 80.2 %all-gather.18.cloned.1.call-start = ((), (), s32[]{:S(2)}) async-start(), calls=%async_computation.14 | async-start | bytes 1114112 | tf_op jit(solution)/shard_map/all_gather | solution.py:86
  7.9 161.4 %all-gather.12.cloned.1.call-start = ((), (), s32[]{:S(2)}) async-start(), calls=%async_computation.11 | async-start | bytes 4718592 | tf_op jit(solution)/shard_map/all_gather | solution.py:73
  79.5 5.9 copy-start.19
  80.7 4.7 copy-start.21
  82.8 137.0 %all-gather.16.cloned.1.call-start = ((), (), s32[]{:S(2)}) async-start(), calls=%async_computation.13 | async-start | bytes 1114112 | tf_op jit(solution)/shard_map/all_gather | solution.py:85
  83.5 182.2 %all-gather.14.cloned.1.call-start = ((), (), s32[]{:S(2)}) async-start(), calls=%async_computation.12 | async-start | bytes 1114112 | tf_op jit(solution)/shard_map/all_gather | solution.py:84
  84.1 227.9 %all-gather.20.cloned.1.call-start = ((), (), s32[]{:S(2)}) async-start(), calls=%async_computation.15 | async-start | bytes 1114112 | tf_op jit(solution)/shard_map/all_gather | solution.py:87
  84.7 320.5 %reduce-scatter.20.cloned.1.call-start = ((), (), s32[]{:S(2)}) async-start(), calls=%async_computation.16 | async-start | bytes 4718592 | tf_op jit(solution)/shard_map/reduce_scatter | solution.py:77
  87.3 186.8 %copy-start.5 = (f32[1024,64]{1,0:T(8,128)}, f32[1024,64]{1,0:T(8,128)S(1)}, u32[]{:S(2)}) copy-start(f32[1024,64]{1,0:T(8,128)S(1)} %get-tuple-element.562) | copy-start | bytes 786436
  87.4 186.8 %copy-start.7 = (f32[1024,64]{1,0:T(8,128)}, f32[1024,64]{1,0:T(8,128)S(1)}, u32[]{:S(2)}) copy-start(f32[1024,64]{1,0:T(8,128)S(1)} %get-tuple-element.563) | copy-start | bytes 786436
  274.1 3.1 copy-start.15
  292.1 19.9 %copy-start.4 = (bf16[1024,2,128]{2,0,1:T(8,128)(2,1)}, bf16[1024,2,128]{2,0,1:T(8,128)(2,1)S(1)}, u32[]{:S(2)}) copy-start(bf16[1024,2,128]{2,0,1:T(8,128)(2,1)S(1)} %get-tuple-element.823) | copy-start | bytes 1572868
  316.5 88.7 %copy-start.1 = (bf16[128,2048]{1,0:T(8,128)(2,1)S(1)}, bf16[128,2048]{1,0:T(8,128)(2,1)}, u32[]{:S(2)}) copy-start(bf16[128,2048]{1,0:T(8,128)(2,1)} %param.16) | copy-start | bytes 1572868
  316.5 145.1 %all-gather.26.cloned.1.call-start = ((), (), s32[]{:S(2)}) async-start(), calls=%async_computation.19 | async-start | bytes 2994176 | tf_op jit(solution)/shard_map/all_gather | solution.py:94
  317.2 234.5 %all-gather.22.cloned.1.call-start = ((), (), s32[]{:S(2)}) async-start(), calls=%async_computation.17 | async-start | bytes 4718592 | tf_op jit(solution)/shard_map/all_gather | solution.py:73
  408.6 201.3 %all-gather.24.cloned.1.call-start = ((), (), s32[]{:S(2)}) async-start(), calls=%async_computation.18 | async-start | bytes 2994176 | tf_op jit(solution)/shard_map/all_gather | solution.py:93
  409.3 254.0 %all-gather.28.cloned.1.call-start = ((), (), s32[]{:S(2)}) async-start(), calls=%async_computation.20 | async-start | bytes 2994176 | tf_op jit(solution)/shard_map/all_gather | solution.py:95
  409.9 343.0 %all-gather.30.cloned.1.call-start = ((), (), s32[]{:S(2)}) async-start(), calls=%async_computation.22 | async-start | bytes 4718592 | tf_op jit(solution)/shard_map/all_gather | solution.py:73
  410.6 462.8 %reduce-scatter.24.cloned.1.call-start = ((), (), s32[]{:S(2)}) async-start(), calls=%async_computation.23 | async-start | bytes 4718592 | tf_op jit(solution)/shard_map/reduce_scatter | solution.py:77
  752.9 10.0 copy-start.24
  762.9 3.6 copy-start.25
  762.9 3.6 copy-start.26
  762.9 3.6 copy-start.23
  780.3 93.0 %copy-start.2 = (bf16[128,2048]{1,0:T(8,128)(2,1)S(1)}, bf16[128,2048]{1,0:T(8,128)(2,1)}, u32[]{:S(2)}) copy-start(bf16[128,2048]{1,0:T(8,128)(2,1)} %reduce-scatter.20.cloned.1.call-done) | copy-start | bytes 1572868
  780.3 94.6 %copy-start.9 = (bf16[128,2048]{1,0:T(8,128)(2,1)S(1)}, bf16[128,2048]{1,0:T(8,128)(2,1)}, u32[]{:S(2)}) copy-start(bf16[128,2048]{1,0:T(8,128)(2,1)} %param.27) | copy-start | bytes 1572868
  780.4 187.7 %all-gather.32.cloned.1.call-start = ((), (), s32[]{:S(2)}) async-start(), calls=%async_computation.24 | async-start | bytes 4718592 | tf_op jit(solution)/shard_map/all_gather | solution.py:73
  877.2 194.7 %reduce-scatter.40.cloned.1.call-start = ((), (), s32[]{:S(2)}) async-start(), calls=%async_computation.32 | async-start | bytes 3342336
  889.2 237.4 %reduce-scatter.36.cloned.1.call-start = ((), (), s32[]{:S(2)}) async-start(), calls=%async_computation.30 | async-start | bytes 3342336
  901.1 303.4 %reduce-scatter.38.cloned.1.call-start = ((), (), s32[]{:S(2)}) async-start(), calls=%async_computation.31 | async-start | bytes 3342336
  913.1 360.0 %reduce-scatter.34.cloned.1.call-start = ((), (), s32[]{:S(2)}) async-start(), calls=%async_computation.29 | async-start | bytes 1114112
  974.9 368.2 %reduce-scatter.32.cloned.1.call-start = ((), (), s32[]{:S(2)}) async-start(), calls=%async_computation.28 | async-start | bytes 1114112 | tf_op jit(solution)/shard_map/reduce_scatter | solution.py:241
  986.2 2.0 copy-start
  1015.2 2.0 copy-start
  1037.2 4.8 copy-start.13
  1037.2 6.4 copy-start.6
  1037.2 6.4 copy-start.8
  1042.1 370.7 %reduce-scatter.28.cloned.1.call-start = ((), (), s32[]{:S(2)}) async-start(), calls=%async_computation.26 | async-start | bytes 1114112 | tf_op jit(solution)/shard_map/reduce_scatter | solution.py:235
  1047.3 4.9 copy-start.12
  1052.0 430.7 %reduce-scatter.30.cloned.1.call-start = ((), (), s32[]{:S(2)}) async-start(), calls=%async_computation.27 | async-start | bytes 1114112 | tf_op jit(solution)/shard_map/reduce_scatter | solution.py:238
  1052.8 4.7 copy-start.17
  1057.4 518.9 %reduce-scatter.26.cloned.1.call-start = ((), (), s32[]{:S(2)}) async-start(), calls=%async_computation.25 | async-start | bytes 4718592 | tf_op jit(solution)/shard_map/reduce_scatter | solution.py:77
  1057.5 1.3 copy-start.18
  1058.8 1.3 copy-start.14
  1058.8 1.4 copy-start.16
  1063.6 1.4 copy-start.27
  1063.6 607.4 %reduce-scatter.22.cloned.1.call-start = ((), (), s32[]{:S(2)}) async-start(), calls=%async_computation.21 | async-start | bytes 4718592 | tf_op jit(solution)/shard_map/reduce_scatter | solution.py:77
  1071.9 504.5 %copy-start.20 = (f32[2048]{0:T(1024)S(1)}, f32[2048]{0:T(1024)}, u32[]{:S(2)}) copy-start(f32[2048]{0:T(1024)} %copy-done.19) | copy-start | bytes 24580
  1071.9 504.5 %copy-start.22 = (f32[128]{0:T(128)S(1)}, f32[128]{0:T(128)}, u32[]{:S(2)}) copy-start(f32[128]{0:T(128)} %copy-done.21) | copy-start | bytes 1540
  1071.9 599.1 %copy-start.3 = (bf16[128,2048]{1,0:T(8,128)(2,1)S(1)}, bf16[128,2048]{1,0:T(8,128)(2,1)}, u32[]{:S(2)}) copy-start(bf16[128,2048]{1,0:T(8,128)(2,1)} %reduce-scatter.20.cloned.1.call-done) | copy-start | bytes 1572868
  1071.9 599.1 %copy-start.10 = (bf16[128,2048]{1,0:T(8,128)(2,1)S(1)}, bf16[128,2048]{1,0:T(8,128)(2,1)}, u32[]{:S(2)}) copy-start(bf16[128,2048]{1,0:T(8,128)(2,1)} %param.27) | copy-start | bytes 1572868
  1071.9 599.1 %copy-start.11 = (bf16[128,2048]{1,0:T(8,128)(2,1)S(1)}, bf16[128,2048]{1,0:T(8,128)(2,1)}, u32[]{:S(2)}) copy-start(bf16[128,2048]{1,0:T(8,128)(2,1)} %reduce-scatter.24.cloned.1.call-done) | copy-start | bytes 1572868
Sparse Core Ops, SparseCore 0:
  10.4 48.8 all-gather.17
  82.9 86.3 all-gather.11
  171.7 48.0 all-gather.15
  222.0 43.6 all-gather.13
  267.9 44.0 all-gather.19
  316.6 88.5 reduce-scatter.19
  407.4 54.1 all-gather.25
  463.8 87.8 all-gather.21
  554.0 55.7 all-gather.23
  611.9 51.3 all-gather.27
  665.0 87.8 all-gather.29
  780.5 92.8 reduce-scatter.23
  877.4 90.6 all-gather.31
  972.0 76.7 reduce-scatter.39
  1052.6 74.0 reduce-scatter.35
  1130.5 73.9 reduce-scatter.37
  1208.2 64.7 reduce-scatter.33
  1277.2 65.8 reduce-scatter.31
  1346.9 65.7 reduce-scatter.27
  1416.9 65.7 reduce-scatter.29
  1485.1 91.2 reduce-scatter.25
  1578.7 92.1 reduce-scatter.21
where the time goes:
time: 1690 us; the launch traced here: 1680 us
  waiting for transfers between devices  1260 us (75%)
  matrix products  165 us (10%)
  blocking collectives  150 us (9%)
  local copies, waits for them, and re-layouts  42.3 us (3%)
  other arithmetic  40.8 us (2%)
    all_gather x4, waiting for transfers between devices, spread_rows(): return lax.all_gather(piece, 'tensor', axis=0, tiled=True)  317 us
    reduce_scatter x4, waiting for transfers between devices, sum_rows(): lax.psum_scatter(partial_sum.astype(jnp.bfloat16), 'tensor', scatter_dime...  285 us
    unnamed x26, waiting for transfers between devices  201 us
    unnamed x2, blocking collectives  150 us
    reduce_scatter x1, waiting for transfers between devices, on_device(): lax.psum_scatter(grad_key.astype(jnp.bfloat16), 'dp', scatter_dimension=0...  68.4 us
    reduce_scatter x1, waiting for transfers between devices, on_device(): lax.psum_scatter(grad_value.astype(jnp.bfloat16), 'dp', scatter_dimension...  68.4 us
    reduce_scatter x1, waiting for transfers between devices, on_device(): lax.psum_scatter(grad_query.astype(jnp.bfloat16), 'dp', scatter_dimension...  68.1 us
    all_gather x1, waiting for transfers between devices, fetch_mlp(): lax.all_gather(w_up, 'dp', axis=0, tiled=True)  51 us
  transfers between devices with their start and end apart: 22, of which 20 were waited for; matrix products, arithmetic and copies ran while one was open for 12% of the time, Pallas kernels for 0%

commit v1 on v0

v1 whole, which is shorter than its diff:
```python
import functools
import math
import types

import jax
import jax.numpy as jnp
import numpy as np
from jax import lax
from jax.experimental import pallas as pl
from jax.experimental.pallas import tpu as pltpu
from jax.sharding import PartitionSpec as P

HD = 128
PIECE = 256
EPS = 1e-05
NEG = -1e30
SCALE = HD ** (-0.5)
D = 2048
SEQ = 1024
UNITS = 688
BF = jnp.bfloat16
F32 = jnp.float32
MESH = pl.DeviceIdType.MESH
VMEM_BYTES = 60 * 1024 * 1024
ALL = slice(None)


def dot_nn(left, right):
    return jnp.dot(left, right, preferred_element_type=F32)


def dot_nt(left, right):
    return lax.dot_general(left, right, (((1,), (1,)), ((), ())), preferred_element_type=F32)


def dot_tn(left, right):
    return lax.dot_general(left, right, (((0,), (0,)), ((), ())), preferred_element_type=F32)


def rem4(value):
    return lax.rem(value, 4)


def place():
    dp = lax.axis_index("dp")
    tp = lax.axis_index("tensor")
    zh = lax.rem(lax.div(dp, 2), 2)
    zl = lax.rem(tp, 2)
    return types.SimpleNamespace(
        y=lax.div(dp, 4), zh=zh, zl=zl, z=zh * 2 + zl, x=lax.div(tp, 2), core=lax.rem(dp, 2)
    )


def device(me, **moved):
    at = types.SimpleNamespace(**{**vars(me), **moved})
    zh, zl = lax.div(at.z, 2), lax.rem(at.z, 2)
    return (at.y * 4 + zh * 2 + at.core, at.x * 2 + zl)


def near(me, axis, step):
    return device(me, **{axis: rem4(getattr(me, axis) + step)})


def sibling(me):
    return device(me, core=1 - me.core)


def partner(me):
    return device(me, z=me.zh * 2 + 1 - me.zl)


def greet(me, axes):
    others = [near(me, axis, step) for axis in axes for step in (1, 3)] + [sibling(me)]
    barrier = pltpu.get_barrier_semaphore()
    for other in others:
        pl.semaphore_signal(barrier, inc=1, device_id=other, device_id_type=MESH)
    pl.semaphore_wait(barrier, len(others))


class Wire:
    def __init__(self, send, recv, local):
        self.send, self.recv, self.local = send, recv, local
        self.used, self.used_local = 0, 0
        self.sent = []

    def put(self, source, target, to):
        index = self.used
        self.used += 1
        copy = pltpu.make_async_remote_copy(
            src_ref=source,
            dst_ref=target,
            send_sem=self.send.at[index],
            recv_sem=self.recv.at[index],
            device_id=to,
            device_id_type=MESH,
        )
        copy.start()
        self.sent.append(copy)
        return copy

    def move(self, source, target):
        index = self.used_local
        self.used_local += 1
        copy = pltpu.make_async_copy(source, target, self.local.at[index])
        copy.start()
        return copy

    def settle(self, copies):
        for copy in copies:
            copy.wait_send()
        done = {id(copy) for copy in copies}
        self.sent = [copy for copy in self.sent if id(copy) not in done]

    def drain(self):
        for copy in self.sent:
            copy.wait_send()
        self.sent = []


class Ring:
    def __init__(self, wire, me, axis, view, own=None):
        self.wire, self.view = wire, view
        self.at = getattr(me, axis)
        self.right, self.left = near(me, axis, 1), near(me, axis, 3)
        self.own = view(self.at, None) if own is None else own

    def start(self):
        target = self.view(self.at, None)
        self.to_right = self.wire.put(self.own, target, self.right)
        self.to_left = self.wire.put(self.own, target, self.left)
        return self

    def relay(self, halves=True):
        before, after = rem4(self.at + 3), rem4(self.at + 1)
        self.to_right.wait_recv()
        piece = self.view(before, 0 if halves else None)
        self.far = [self.wire.put(piece, piece, self.right)]
        self.to_left.wait_recv()
        if halves:
            piece = self.view(after, 1)
            self.far.append(self.wire.put(piece, piece, self.left))
        return self

    def finish(self):
        for copy in self.far:
            copy.wait_recv()
        return self


def add_rows(target, terms, rows, step):
    def body(index, carry):
        span = pl.ds(pl.multiple_of(index * step, step), step)
        total = terms[0][span, :].astype(F32)
        for term in terms[1:]:
            total = total + term[span, :].astype(F32)
        target[span, :] = total.astype(target.dtype)
        return carry

    lax.fori_loop(0, rows // step, body, 0)


class RingSum:
    def __init__(self, wire, me, axis, part, from_left, from_right, whole_left, whole_right, add):
        self.wire, self.part, self.add = wire, part, add
        self.at = getattr(me, axis)
        self.right, self.left = near(me, axis, 1), near(me, axis, 3)
        self.near_bufs = (from_left, from_right)
        self.whole = (whole_left, whole_right)

    def start(self, halves=(0, 1)):
        far = rem4(self.at + 2)
        if 0 in halves:
            self.first = self.wire.put(self.part(far, 0), self.near_bufs[0], self.right)
        if 1 in halves:
            self.second = self.wire.put(self.part(far, 1), self.near_bufs[1], self.left)
        return self

    def relay(self):
        after, before = rem4(self.at + 1), rem4(self.at + 3)
        self.first.wait_recv()
        self.add(self.part(after, 0), self.near_bufs[0])
        self.to_right = self.wire.put(self.part(after, None), self.whole[0], self.right)
        self.second.wait_recv()
        self.add(self.part(before, 1), self.near_bufs[1])
        self.to_left = self.wire.put(self.part(before, None), self.whole[1], self.left)
        return self

    def finish(self):
        self.to_right.wait_recv()
        self.to_left.wait_recv()
        return self


class Spread:
    def __init__(self, wire, me, ref, lead, row, rows, first, cut, source):
        self.wire, self.me, self.first = wire, me, first
        head = (ALL,) * lead

        def view(y, z, part):
            zl, zh = (ALL, ALL) if z is None else (lax.rem(z, 2), lax.div(z, 2))
            start, size = row, rows
            if part == 0:
                size = cut
            if part == 1:
                start, size = row + cut, rows - cut
            yy = ALL if y is None else y
            return ref.at[head + (zl, yy, zh, me.core, pl.ds(start, size), ALL)]

        self.view = view
        own = source.at[head + (pl.ds(row, rows), ALL)]
        if first == "y":
            self.one = Ring(wire, me, "y", lambda slot, part: view(slot, me.z, part), own)
            self.two = Ring(wire, me, "z", lambda slot, part: view(None, slot, part))
        else:
            self.one = Ring(wire, me, "z", lambda slot, part: view(me.y, slot, part), own)
            self.two = Ring(wire, me, "y", lambda slot, part: view(slot, None, part))

    def core(self):
        piece = self.view(None, None, None)
        self.last = self.wire.put(piece, piece, sibling(self.me))
        return self


def norm_rows(source, target, gain, rows, step=32):
    def body(index, carry):
        span = pl.ds(pl.multiple_of(index * step, step), step)
        value = source[span, :].astype(F32)
        scale = lax.rsqrt(jnp.mean(value * value, axis=-1, keepdims=True) + EPS)
        target[span, :] = (value * scale * gain).astype(BF)
        return carry

    lax.fori_loop(0, rows // step, body, 0)


def fill_bias(bias, me, start):
    row = lax.broadcasted_iota(jnp.int32, (128, 512), 0)
    column = lax.broadcasted_iota(jnp.int32, (128, 512), 1)
    query = lax.div(column, 128) * 256 + me.zl * 128 + lax.rem(column, 128)
    query_in = (query >= start) & (query < start + PIECE)

    def body(block, carry):
        pair, other = lax.div(block, 2), lax.rem(block, 2)
        parity = me.zl + other * (1 - 2 * me.zl)
        key = (pair * 2 + parity) * 128 + row
        key_in = (key >= start) & (key < start + PIECE)
        allowed = (key <= query) | (query_in & key_in)
        bias[pl.ds(pl.multiple_of(block * 128, 128), 128), :] = jnp.where(allowed, 0.0, NEG)
        return carry

    lax.fori_loop(0, 8, body, 0)


def turn(field, cosine, sine):
    return field * cosine + pltpu.roll(field, HD // 2, 1) * sine


def kernel_attend(
    tokens_in, cotangent_in, start_in, qkv_in, out_in, wide_in, down_in, tile_in, tables_in,
    qkv_out, wo_out, wide_out, down_out, cot_out, turned_out,
    query_out, keys_out, values_out, heads_out, lse_out, y_out, h_out, gains_out,
    tok, h_one, w_qkv, w_o, tables, bias, part, near_left, near_right, whole_left, whole_right,
    turned, gain_x, gain_z, gain_y, gain_c,
    send, recv, local,
):
    me = place()
    wire = Wire(send, recv, local)
    greet(me, ("x", "y", "z"))
    one = rem4(me.x + 1)
    three = rem4(me.x + 3)

    rows_x = Ring(
        wire, me, "x",
        lambda slot, half: tok.at[slot, 0] if half is None else tok.at[slot, 0, pl.ds(half * 64, 64)],
        tokens_in,
    ).start()
    rows_z = wire.put(tokens_in, tok.at[me.x, 1], partner(me))
    gain_ring_x = Ring(wire, me, "x", lambda slot, half: gain_x.at[slot], tile_in).start()
    qkv = [
        Spread(wire, me, w_qkv, 1, 0, 64, "y", 32, qkv_in),
        Spread(wire, me, w_qkv, 1, 64, 64, "z", 32, qkv_in),
    ]
    for item in qkv:
        item.one.start()
    own = [
        wire.move(tokens_in, tok.at[me.x, 0]),
        wire.move(tile_in, gain_x.at[me.x]),
        wire.move(qkv_in, w_qkv.at[:, me.zl, me.y, me.zh, me.core]),
        wire.move(out_in, w_o.at[me.zl, me.y, me.zh, me.core]),
        wire.move(wide_in, wide_out.at[:, me.zl, me.y, me.zh, me.core]),
        wire.move(down_in, down_out.at[me.zl, me.y, me.zh, me.core]),
        wire.move(tables_in.at[me.zl], tables),
        wire.move(cotangent_in, cot_out.at[me.x]),
    ]
    fill_bias(bias, me, start_in[0])
    for copy in own:
        copy.wait()

    gain_ring_x.relay(False)
    rows_x.relay()
    rows_z.wait_recv()
    other_right = wire.put(tok.at[me.x, 1], tok.at[me.x, 1], near(me, "x", 1))
    other_left = wire.put(tok.at[me.x, 1], tok.at[me.x, 1], near(me, "x", 3))
    for item in qkv:
        item.one.relay()
    gain_ring_x.finish()
    gain_z[me.z] = gain_x[0] + gain_x[1] + gain_x[2] + gain_x[3]
    gain_ring_z = Ring(wire, me, "z", lambda slot, half: gain_z.at[slot]).start()
    for item in qkv:
        item.one.finish()
        item.two.start()
    later = [
        Spread(wire, me, w_o, 0, 0, 128, "y", 64, out_in),
        Spread(wire, me, w_o, 0, 128, 128, "z", 64, out_in),
        Spread(wire, me, wide_out, 1, 0, 64, "y", 32, wide_in),
        Spread(wire, me, wide_out, 1, 64, 64, "z", 32, wide_in),
        Spread(wire, me, down_out, 0, 0, 352, "y", 176, down_in),
        Spread(wire, me, down_out, 0, 352, 336, "z", 176, down_in),
    ]
    for item in later:
        item.one.start()
    gain_ring_z.relay(False).finish()
    gain_y[me.y, 0] = gain_z[0] + gain_z[1]
    gain_y[me.y, 1] = gain_z[2] + gain_z[3]
    gain_ring_y = Ring(wire, me, "y", lambda slot, half: gain_y.at[slot]).start()
    gain_ring_y.relay(False).finish()
    gain_c[me.core] = gain_y[...]
    piece = gain_c.at[me.core]
    wire.put(piece, piece, sibling(me)).wait_recv()
    for y in range(4):
        for zh in range(2):
            for core in range(2):
                column = (y * 4 + zh * 2 + core) * 128
                gains_out[:, column : column + 128] = gain_c[core, y, zh]
    gain_one, gain_two = gains_out[0:1, :], gains_out[1:2, :]

    norm_rows(tok.at[me.x, 0], h_one.at[me.x, 0], gain_one, 128)
    norm_rows(tok.at[me.x, 1], h_one.at[me.x, 1], gain_one, 128)
    norm_rows(tok.at[one, 0], h_one.at[one, 0], gain_one, 128)
    norm_rows(tok.at[three, 0], h_one.at[three, 0], gain_one, 128)
    for item in qkv:
        item.two.relay()
    rows_x.finish()
    far = rem4(me.x + 2)
    far_z = wire.put(tok.at[far, 0], tok.at[far, 1], partner(me))
    norm_rows(tok.at[far, 0], h_one.at[far, 0], gain_one, 128)
    other_right.wait_recv()
    other_left.wait_recv()
    norm_rows(tok.at[one, 1], h_one.at[one, 1], gain_one, 128)
    norm_rows(tok.at[three, 1], h_one.at[three, 1], gain_one, 128)
    cot_x = Ring(
        wire, me, "x",
        lambda slot, half: cot_out.at[slot] if half is None else cot_out.at[slot, pl.ds(half * 64, 64)],
        cotangent_in,
    ).start()
    for item in qkv:
        item.two.finish()
        item.core()
    for item in later:
        item.one.relay()
    far_z.wait_recv()
    norm_rows(tok.at[far, 1], h_one.at[far, 1], gain_one, 128)
    for item in qkv:
        item.last.wait_recv()
    kept = [wire.move(w_qkv, qkv_out)]
    for item in later:
        item.one.finish()
        item.two.start()

    def project(pair, carry):
        def weight(which):
            return w_qkv[which, pair].reshape(D, 256)

        raw = dot_nn(h_one[:, 0].reshape(512, D), weight(0))
        for j in range(2):
            cosine = tables[0, :, 0].reshape(512, HD)
            sine = tables[1, :, 0].reshape(512, HD)
            query_out[pair * 2 + j] = turn(raw[:, j * HD : (j + 1) * HD], cosine, sine).astype(BF)
        for half in range(2):
            rows = h_one[2 * half : 2 * half + 2].reshape(512, D)
            span = slice(half * 512, half * 512 + 512)
            raw = dot_nn(rows, weight(1))
            cosine = tables[0, 2 * half : 2 * half + 2].reshape(512, HD)
            sine = tables[1, 2 * half : 2 * half + 2].reshape(512, HD)
            for j in range(2):
                keys_out[pair * 2 + j, span, :] = turn(
                    raw[:, j * HD : (j + 1) * HD], cosine, sine
                ).astype(BF)
            raw = dot_nn(rows, weight(2))
            for j in range(2):
                values_out[pair * 2 + j, span, :] = raw[:, j * HD : (j + 1) * HD].astype(BF)
        return carry

    lax.fori_loop(0, 2, project, 0)
    cot_x.relay()

    def attend(head, carry):
        for half, span in ((0, 768), (1, 1024)):
            rows = slice(half * 256, half * 256 + 256)
            scores = dot_nt(keys_out[head, 0:span, :], query_out[head, rows, :]) * SCALE
            scores = scores + bias[0:span, rows]
            top = jnp.max(scores, axis=0, keepdims=True)
            expo = jnp.exp(scores - top)
            total = jnp.sum(expo, axis=0, keepdims=True)
            probs = (expo * (1.0 / total)).astype(BF)
            result = dot_tn(values_out[head, 0:span, :], probs)
            heads_out[rows, pl.ds(pl.multiple_of(head * HD, HD), HD)] = result.T.astype(BF)
            lse_out[head, :, rows] = top + jnp.log(total)
        return carry

    lax.fori_loop(0, 4, attend, 0)
    for item in later:
        item.two.relay()

    def project_out(block, carry):
        y, zh = lax.div(block, 2), lax.rem(block, 2)
        weight = jnp.concatenate(
            [
                jnp.concatenate([w_o[zl, y, zh, 0], w_o[zl, y, zh, 1]], axis=1)
                for zl in range(2)
            ],
            axis=0,
        )
        result = dot_nn(heads_out[...], weight).astype(BF).reshape(4, 128, 256)
        part[:, :, pl.ds(pl.multiple_of(block * 256, 256), 256)] = result
        return carry

    later[0].two.finish()
    later[1].two.finish()
    later[0].core()
    later[1].core()
    later[0].last.wait_recv()
    later[1].last.wait_recv()
    kept.append(wire.move(w_o, wo_out))
    cot_x.finish()

    def halves(ref):
        def view(slot, half):
            if half is None:
                return ref.at[slot]
            return ref.at[slot, :, pl.ds(half * 1024, 1024)]

        return view

    total = RingSum(
        wire, me, "x", halves(part), near_left, near_right, whole_left, whole_right,
        lambda target, term: add_rows(target, [target, term], 128, 32),
    )
    lax.fori_loop(0, 4, project_out, 0)
    total.start((0,))
    lax.fori_loop(4, 8, project_out, 0)
    total.start((1,))

    def flip(block, carry):
        column = pl.ds(pl.multiple_of(block * 128, 128), 128)
        rows = h_one[:, :, :, column].reshape(SEQ, 128)
        turned[lax.rem(block, 2), lax.div(block, 2)] = rows.T
        return carry

    lax.fori_loop(0, 8, flip, 0)
    total.relay()
    lax.fori_loop(8, 16, flip, 0)
    kept.append(wire.move(turned.at[me.core], turned_out.at[0]))
    turned_far = wire.put(turned.at[1 - me.core], turned_out.at[1], sibling(me))
    for item in later[2:]:
        item.two.finish()
        item.core()
    total.finish()

    def finish(index, carry):
        span = pl.ds(pl.multiple_of(index * 32, 32), 32)
        value = tok[me.x, 0, span, :].astype(F32) + (
            part[me.x, span, :].astype(F32)
            + whole_left[span, :].astype(F32)
            + whole_right[span, :].astype(F32)
        )
        scale = lax.rsqrt(jnp.mean(value * value, axis=-1, keepdims=True) + EPS)
        y_out[span, :] = value
        h_out[span, :] = (value * scale * gain_two).astype(BF)
        return carry

    lax.fori_loop(0, 4, finish, 0)
    for item in later[2:]:
        item.last.wait_recv()
    turned_far.wait_recv()
    for copy in kept:
        copy.wait()
    wire.drain()


def anywhere():
    return pl.BlockSpec(memory_space=pl.ANY)


def in_vmem():
    return pl.BlockSpec(memory_space=pltpu.VMEM)


def call_attend(tokens, cotangent, starts, qkv, w_out, wide, w_down, tile, tables):
    shape = jax.ShapeDtypeStruct
    return pl.pallas_call(
        kernel_attend,
        name="attend",
        in_specs=[anywhere(), anywhere(), pl.BlockSpec(memory_space=pltpu.SMEM)] + [anywhere()] * 6,
        out_specs=[anywhere()] * 6 + [in_vmem()] * 8,
        out_shape=[
            shape((3, 2, 4, 2, 2, 128, 256), BF),
            shape((2, 4, 2, 2, 256, 128), BF),
            shape((2, 2, 4, 2, 2, 128, UNITS), BF),
            shape((2, 4, 2, 2, UNITS, 128), BF),
            shape((4, 128, D), BF),
            shape((2, 8, 128, SEQ), BF),
            shape((4, 512, HD), BF),
            shape((4, SEQ, HD), BF),
            shape((4, SEQ, HD), BF),
            shape((512, 512), BF),
            shape((4, 1, 512), F32),
            shape((128, D), F32),
            shape((128, D), BF),
            shape((8, D), F32),
        ],
        scratch_shapes=[
            pltpu.VMEM((4, 2, 128, D), BF),
            pltpu.VMEM((4, 2, 128, D), BF),
            pltpu.VMEM((3, 2, 4, 2, 2, 128, 256), BF),
            pltpu.VMEM((2, 4, 2, 2, 256, 128), BF),
            pltpu.VMEM((2, 4, 2, 128, HD), F32),
            pltpu.VMEM((SEQ, 512), F32),
            pltpu.VMEM((4, 128, D), BF),
            pltpu.VMEM((128, D // 2), BF),
            pltpu.VMEM((128, D // 2), BF),
            pltpu.VMEM((128, D), BF),
            pltpu.VMEM((128, D), BF),
            pltpu.VMEM((2, 8, 128, SEQ), BF),
            pltpu.VMEM((4, 8, 128), F32),
            pltpu.VMEM((4, 8, 128), F32),
            pltpu.VMEM((4, 2, 8, 128), F32),
            pltpu.VMEM((2, 4, 2, 8, 128), F32),
            pltpu.SemaphoreType.DMA((110,)),
            pltpu.SemaphoreType.DMA((110,)),
            pltpu.SemaphoreType.DMA((16,)),
        ],
        compiler_params=pltpu.CompilerParams(
            collective_id=0, has_side_effects=True, vmem_limit_bytes=VMEM_BYTES
        ),
    )(tokens, cotangent, starts, qkv, w_out, wide, w_down, tile, tables)


def rope_tables():
    half = HD // 2
    freq = np.exp(np.arange(half, dtype=np.float32) * np.float32(-2.0 * math.log(10000.0) / HD))
    order = np.array(
        [
            [[(2 * pair + (zl + other) % 2) * 128 + np.arange(128) for other in range(2)] for pair in range(4)]
            for zl in range(2)
        ]
    )
    angle = order.astype(np.float32)[..., None] * freq.astype(np.float32)
    cosine, sine = np.cos(angle.astype(np.float64)), np.sin(angle.astype(np.float64))
    both = np.stack(
        [np.concatenate([cosine, cosine], -1), np.concatenate([-sine, sine], -1)], axis=1
    )
    return both.astype(np.float32)


def gain_tile(gain_attn, gain_mlp):
    column = lax.axis_index("tensor") * 16
    both = jnp.stack([gain_attn, gain_mlp])
    return lax.dynamic_update_slice(jnp.zeros((8, 128), F32), both, (0, column))


def add_into(target, terms, result=None):
    shape = target.shape
    lead, rows, columns = shape[:-2], shape[-2], shape[-1]
    step = rows
    while step * columns > 33000:
        step = next(s for s in range(step - 16, 0, -16) if rows % s == 0)
    cuts = rows // step
    result = target if result is None else result

    def body(index, carry):
        where, rest = [], lax.div(index, cuts)
        for extent in reversed(lead):
            where.insert(0, lax.rem(rest, extent))
            rest = lax.div(rest, extent)
        where = tuple(where) + (
            pl.ds(pl.multiple_of(lax.rem(index, cuts) * step, 16), step), ALL
        )
        total = target[where].astype(F32)
        for term in terms:
            total = total + term[where].astype(F32)
        result[where] = total.astype(result.dtype)
        return carry

    lax.fori_loop(0, math.prod(lead) * cuts, body, 0)


def columns_of(ref):
    def view(slot, half):
        if half is None:
            return ref.at[slot]
        return ref.at[slot, :, pl.ds(half * (D // 2), D // 2)]

    return view


def rows_of(ref):
    def view(slot, half):
        return ref.at[slot] if half is None else ref.at[slot, pl.ds(half * 64, 64)]

    return view


def fold_view(ref, me, lead, axis, row, rows, cut):
    head = (ALL,) * lead

    def view(slot, part):
        start, size = row, rows
        if part == 0:
            size = cut
        if part == 1:
            start, size = row + cut, rows - cut
        if axis == "y":
            where = (ALL, slot, ALL)
        else:
            where = (lax.rem(slot, 2), ALL, lax.div(slot, 2))
        return ref.at[head + where + (pl.ds(start, size), ALL)]

    return view


def kernel_feed(
    h_in, cot_in, wide_in, down_in, y_in, gains_in,
    part_out, dattn_out, wide_y_out, wide_z_out, down_y_out, down_z_out, dy_out, gain_out,
    w_wide, w_down, h_two, cot, gate_s, up_s, act_s, d_wide, act, act_t, d_wide_far, act_t_far,
    h_t, h_t_far, cot_far, part, near_left, near_right, whole_left, whole_right, d_attn,
    wy_near_left, wy_near_right, wy_left, wy_right, wz_near_left, wz_near_right, wz_left, wz_right,
    dy_near_left, dy_near_right, dy_left, dy_right, dz_near_left, dz_near_right, dz_left, dz_right,
    send, recv, local,
):
    me = place()
    wire = Wire(send, recv, local)
    greet(me, ("x", "y", "z"))
    h_ring = Ring(wire, me, "x", rows_of(h_two), h_in).start()
    loads = [
        wire.move(cot_in, cot),
        wire.move(down_in, w_down),
        wire.move(h_in, h_two.at[me.x]),
        wire.move(wide_in, w_wide),
    ]
    loads[0].wait()
    cot_puts = []
    for block in range(8):
        column = pl.ds(pl.multiple_of((block * 2 + 1 - me.core) * 128, 128), 128)
        cot_puts.append(wire.put(cot.at[:, :, column], cot_far.at[block], sibling(me)))
    loads[1].wait()

    def back_act(zl, carry):
        weight = jnp.concatenate(
            [w_down[zl, y, zh, c] for y in range(4) for zh in range(2) for c in range(2)], axis=1
        )
        act_s[zl] = dot_nt(cot[...].reshape(512, D), weight)
        return carry

    lax.fori_loop(0, 1, back_act, 0)
    h_ring.relay()
    lax.fori_loop(1, 2, back_act, 0)
    loads[2].wait()
    loads[3].wait()
    h_ring.finish()

    def forward(zl, carry):
        rows = h_two[...].reshape(512, D)
        gate_s[...] = dot_nn(rows, w_wide[0, zl].reshape(D, UNITS))
        up_s[...] = dot_nn(rows, w_wide[1, zl].reshape(D, UNITS))

        def inner(index, carry):
            span = pl.ds(pl.multiple_of(index * 32, 32), 32)
            gate, up, d_act = gate_s[span, :], up_s[span, :], act_s[zl, span, :]
            sigma = 1.0 / (1.0 + jnp.exp(-gate))
            act[zl, span, :] = (gate * sigma * up).astype(BF)
            d_wide[0, zl, span, :] = (d_act * up * sigma * (1.0 + gate * (1.0 - sigma))).astype(BF)
            d_wide[1, zl, span, :] = (d_act * gate * sigma).astype(BF)
            return carry

        lax.fori_loop(0, 16, inner, 0)
        act_t[zl] = act[zl].T
        return carry

    lax.fori_loop(0, 2, forward, 0)

    def flip(block, carry):
        column = pl.ds(pl.multiple_of(block * 128, 128), 128)
        h_t[lax.rem(block, 2), lax.div(block, 2)] = h_two[:, :, column].reshape(512, 128).T
        return carry

    lax.fori_loop(0, 16, flip, 0)
    far = [
        wire.put(h_t.at[1 - me.core], h_t_far, sibling(me)),
        wire.put(d_wide, d_wide_far, sibling(me)),
        wire.put(act_t, act_t_far, sibling(me)),
    ]

    def back_h(block, carry):
        y, zh = lax.div(block, 2), lax.rem(block, 2)
        total = None
        for which in range(2):
            for zl in range(2):
                weight = w_wide[which, zl, y, zh].reshape(256, UNITS)
                term = dot_nt(d_wide[which, zl], weight)
                total = term if total is None else total + term
        part[:, :, pl.ds(pl.multiple_of(block * 256, 256), 256)] = total.astype(BF).reshape(4, 128, 256)
        return carry

    total = RingSum(
        wire, me, "x", columns_of(part), near_left, near_right, whole_left, whole_right,
        lambda target, term: add_into(target, [term]),
    )
    lax.fori_loop(0, 4, back_h, 0)
    total.start((0,))
    lax.fori_loop(4, 8, back_h, 0)
    total.start((1,))
    wire.settle((h_ring.to_right, h_ring.to_left, *h_ring.far))

    def forward_down(block, carry):
        y, zh = lax.div(block, 2), lax.rem(block, 2)
        result = None
        for zl in range(2):
            weight = jnp.concatenate([w_down[zl, y, zh, 0], w_down[zl, y, zh, 1]], axis=1)
            term = dot_nn(act[zl], weight)
            result = term if result is None else result + term
        h_two[:, :, pl.ds(pl.multiple_of(block * 256, 256), 256)] = result.astype(BF).reshape(4, 128, 256)
        return carry

    lax.fori_loop(0, 8, forward_down, 0)
    kept = [wire.move(h_two, part_out)]
    total.relay()
    for copy in far[:2]:
        copy.wait_recv()

    def grad_wide(index, carry):
        which, rest = lax.div(index, 4), lax.rem(index, 4)
        zl, pair = lax.div(rest, 2), lax.rem(rest, 2)
        blocks = pl.ds(pair * 4, 4)
        result = dot_nn(h_t[me.core, blocks].reshape(512, 512), d_wide[which, zl]) + dot_nn(
            h_t_far[blocks].reshape(512, 512), d_wide_far[which, zl]
        )
        w_wide[which, zl, pl.ds(pair * 2, 2), :, 0] = result.astype(BF).reshape(2, 2, 128, UNITS)
        return carry

    lax.fori_loop(0, 8, grad_wide, 0)
    g_wide = w_wide.at[:, :, :, :, 0]
    g_down = w_down.at[:, :, :, 0]

    def add(target, term):
        add_into(target, [term])

    sums = [
        RingSum(wire, me, "y", fold_view(g_wide, me, 1, "y", 0, 64, 32),
                wy_near_left, wy_near_right, wy_left, wy_right, add),
        RingSum(wire, me, "z", fold_view(g_wide, me, 1, "z", 64, 64, 32),
                wz_near_left, wz_near_right, wz_left, wz_right, add),
    ]
    for item in sums:
        item.start()
    total.finish()

    gain_two = gains_in[1:2, :]

    def back_norm(index, carry):
        span = pl.ds(pl.multiple_of(index * 16, 16), 16)
        d_h = (
            part[me.x, span, :].astype(F32)
            + whole_left[span, :].astype(F32)
            + whole_right[span, :].astype(F32)
        )
        value = y_in[span, :]
        scale = lax.rsqrt(jnp.mean(value * value, axis=-1, keepdims=True) + EPS)
        normed = value * scale
        e_two = d_h * gain_two
        inner = jnp.mean(e_two * normed, axis=-1, keepdims=True)
        d_y = cot[me.x, span, :].astype(F32) + scale * (e_two - normed * inner)
        dy_out[span, :] = d_y
        d_attn[span, :] = d_y.astype(BF)
        return carry + jnp.sum(d_h * normed, axis=0, keepdims=True)

    gain_out[0:1, :] = lax.fori_loop(0, 8, back_norm, jnp.zeros((1, D), F32))
    d_ring = Ring(wire, me, "x", rows_of(dattn_out), d_attn).start()
    kept.append(wire.move(d_attn, dattn_out.at[me.x]))
    far[2].wait_recv()
    for copy in cot_puts:
        copy.wait_recv()

    def grad_down(index, carry):
        zl, y = lax.div(index, 4), lax.rem(index, 4)
        mine = jnp.concatenate(
            [
                cot[:, :, pl.ds(pl.multiple_of(((y * 2 + zh) * 2 + me.core) * 128, 128), 128)]
                .reshape(512, 128)
                for zh in range(2)
            ],
            axis=1,
        )
        other = jnp.concatenate(
            [cot_far[y * 2 + zh].reshape(512, 128) for zh in range(2)], axis=1
        )
        result = (dot_nn(act_t[zl], mine) + dot_nn(act_t_far[zl], other)).astype(BF)
        w_down[zl, y, 0, 0] = result[:, 0:128]
        w_down[zl, y, 1, 0] = result[:, 128:256]
        return carry

    lax.fori_loop(0, 8, grad_down, 0)
    sums += [
        RingSum(wire, me, "y", fold_view(g_down, me, 0, "y", 0, 352, 176),
                dy_near_left, dy_near_right, dy_left, dy_right, add),
        RingSum(wire, me, "z", fold_view(g_down, me, 0, "z", 352, 336, 176),
                dz_near_left, dz_near_right, dz_left, dz_right, add),
    ]
    for item in sums[2:]:
        item.start()
    for item in sums[:2]:
        item.relay()
    d_ring.relay()
    for item in sums[2:]:
        item.relay()
    outs = (wide_y_out, wide_z_out, down_y_out, down_z_out)
    for item, out in zip(sums, outs):
        item.finish()
        mine = item.part(item.at, None)
        add_into(mine, list(item.whole))
        kept.append(wire.move(mine, out))
    d_ring.finish()
    for copy in kept:
        copy.wait()
    wire.drain()


def call_feed(h_two, cot, wide, down, y_one, gains):
    shape = jax.ShapeDtypeStruct
    return pl.pallas_call(
        kernel_feed,
        name="feed",
        in_specs=[anywhere()] * 4 + [in_vmem()] * 2,
        out_specs=[anywhere()] * 6 + [in_vmem()] * 2,
        out_shape=[
            shape((4, 128, D), BF),
            shape((4, 128, D), BF),
            shape((2, 2, 2, 64, UNITS), BF),
            shape((2, 4, 64, UNITS), BF),
            shape((2, 2, 352, 128), BF),
            shape((4, 336, 128), BF),
            shape((128, D), F32),
            shape((1, D), F32),
        ],
        scratch_shapes=[
            pltpu.VMEM((2, 2, 4, 2, 2, 128, UNITS), BF),
            pltpu.VMEM((2, 4, 2, 2, UNITS, 128), BF),
            pltpu.VMEM((4, 128, D), BF),
            pltpu.VMEM((4, 128, D), BF),
            pltpu.VMEM((512, UNITS), F32),
            pltpu.VMEM((512, UNITS), F32),
            pltpu.VMEM((2, 512, UNITS), F32),
            pltpu.VMEM((2, 2, 512, UNITS), BF),
            pltpu.VMEM((2, 512, UNITS), BF),
            pltpu.VMEM((2, UNITS, 512), BF),
            pltpu.VMEM((2, 2, 512, UNITS), BF),
            pltpu.VMEM((2, UNITS, 512), BF),
            pltpu.VMEM((2, 8, 128, 512), BF),
            pltpu.VMEM((8, 128, 512), BF),
            pltpu.VMEM((8, 4, 128, 128), BF),
            pltpu.VMEM((4, 128, D), BF),
            pltpu.VMEM((128, D // 2), BF),
            pltpu.VMEM((128, D // 2), BF),
            pltpu.VMEM((128, D), BF),
            pltpu.VMEM((128, D), BF),
            pltpu.VMEM((128, D), BF),
            pltpu.VMEM((2, 2, 2, 32, UNITS), BF),
            pltpu.VMEM((2, 2, 2, 32, UNITS), BF),
            pltpu.VMEM((2, 2, 2, 64, UNITS), BF),
            pltpu.VMEM((2, 2, 2, 64, UNITS), BF),
            pltpu.VMEM((2, 4, 32, UNITS), BF),
            pltpu.VMEM((2, 4, 32, UNITS), BF),
            pltpu.VMEM((2, 4, 64, UNITS), BF),
            pltpu.VMEM((2, 4, 64, UNITS), BF),
            pltpu.VMEM((2, 2, 176, 128), BF),
            pltpu.VMEM((2, 2, 176, 128), BF),
            pltpu.VMEM((2, 2, 352, 128), BF),
            pltpu.VMEM((2, 2, 352, 128), BF),
            pltpu.VMEM((4, 176, 128), BF),
            pltpu.VMEM((4, 160, 128), BF),
            pltpu.VMEM((4, 336, 128), BF),
            pltpu.VMEM((4, 336, 128), BF),
            pltpu.SemaphoreType.DMA((60,)),
            pltpu.SemaphoreType.DMA((60,)),
            pltpu.SemaphoreType.DMA((16,)),
        ],
        compiler_params=pltpu.CompilerParams(
            collective_id=1, has_side_effects=True, vmem_limit_bytes=VMEM_BYTES
        ),
    )(h_two, cot, wide, down, y_one, gains)


class Fold:
    def __init__(self, wire, me, view_one, axes, bufs, view_two, bufs_two):
        def add(target, term):
            add_into(target, [term])

        self.wire, self.me, self.axes, self.add = wire, me, axes, add
        self.view_two, self.bufs_two = view_two, bufs_two
        self.one = None
        if view_one is not None:
            self.one = RingSum(wire, me, axes[0], view_one, *bufs, add)

    def start(self):
        self.one.start()

    def relay(self):
        self.one.relay()

    def turn(self):
        if self.one is not None:
            self.one.finish()
            add_into(self.one.part(self.one.at, None), list(self.one.whole))
        self.two = RingSum(self.wire, self.me, self.axes[1], self.view_two, *self.bufs_two, self.add)
        self.two.start()

    def relay_two(self):
        self.two.relay()

    def finish(self, result):
        self.two.finish()
        add_into(self.two.part(self.two.at, None), list(self.two.whole), result)


def crossed_view(ref, me, lead, axis, row, rows, cut):
    head = (ALL,) * lead

    def view(slot, part):
        start, size = row, rows
        if part == 0:
            size = cut
        if part == 1:
            start, size = row + cut, rows - cut
        if axis == "z":
            where = (lax.rem(slot, 2), me.y, lax.div(slot, 2))
        else:
            where = (me.zl, slot, me.zh)
        return ref.at[head + where + (pl.ds(start, size), ALL)]

    return view


def held_view(ref, lead, axis, rows, cut):
    head = (ALL,) * lead

    def view(slot, part):
        start, size = 0, rows
        if part == 0:
            size = cut
        if part == 1:
            start, size = cut, rows - cut
        where = (lax.rem(slot, 2), lax.div(slot, 2)) if axis == "z" else (slot,)
        return ref.at[head + where + (pl.ds(start, size), ALL)]

    return view


def fold_shapes(lead, count, rows, cut, columns):
    return [
        pltpu.VMEM((*lead, *count, cut, columns), BF),
        pltpu.VMEM((*lead, *count, rows - cut, columns), BF),
        pltpu.VMEM((*lead, *count, rows, columns), BF),
        pltpu.VMEM((*lead, *count, rows, columns), BF),
    ]


def kernel_back(
    start_in, tokens_in, dattn_in, part_in, qkv_in, wo_in, query_in, keys_in, values_in, heads_in,
    lse_in, turned_in, tables_in, gains_in, y_in, dy_in, gain_in, wide_y_in, wide_z_in, down_y_in, down_z_in,
    result_out, tokens_out, g_qkv_out, g_o_out, g_wide_out, g_down_out, gains_out,
    w_qkv, w_o, d_attn, out_part, tables, bias, tok, turned, d_heads, d_query, d_keys, d_values,
    d_query_far, d_keys_far, d_values_far, sum_keys, sum_values, heads_t, heads_t_far, attn_far,
    d_h, far_one, side_left, side_right, last_z,
    near_left, near_right, whole_left, whole_right,
    out_near_left, out_near_right, out_whole_left, out_whole_right,
    g_qkv, g_o, wide_y, wide_z, down_y, down_z, gain_t, gain_x, gain_y, gain_z, gain_c,
    *rest,
):
    bufs, (send, recv, local) = list(rest[:-3]), rest[-3:]
    bufs = [tuple(bufs[4 * i : 4 * i + 4]) for i in range(len(bufs) // 4)]
    me = place()
    wire = Wire(send, recv, local)
    greet(me, ("x", "y", "z"))
    loads = [
        wire.move(dattn_in, d_attn),
        wire.move(wo_in, w_o),
        wire.move(wide_y_in, wide_y),
        wire.move(wide_z_in, wide_z),
        wire.move(down_y_in, down_y),
        wire.move(down_z_in, down_z),
        wire.move(part_in, out_part),
        wire.move(tables_in.at[me.zl], tables),
        wire.move(qkv_in, w_qkv),
        wire.move(tokens_in, tok),
        wire.move(turned_in, turned),
    ]
    for copy in loads[2:6]:
        copy.wait()
    feed = [
        Fold(wire, me, None, ("y", "z"), None, held_view(wide_y, 2 - 1, "z", 64, 32), bufs[0]),
        Fold(wire, me, None, ("z", "y"), None, held_view(wide_z, 1, "y", 64, 32), bufs[1]),
        Fold(wire, me, None, ("y", "z"), None, held_view(down_y, 0, "z", 352, 176), bufs[2]),
        Fold(wire, me, None, ("z", "y"), None, held_view(down_z, 0, "y", 336, 176), bufs[3]),
    ]
    for item in feed:
        item.turn()
    loads[0].wait()
    attn_puts = []
    for block in range(8):
        column = pl.ds(pl.multiple_of((block * 2 + 1 - me.core) * 128, 128), 128)
        attn_puts.append(wire.put(d_attn.at[:, :, column], attn_far.at[block], sibling(me)))
    heads_t[...] = heads_in[...].T
    heads_put = wire.put(heads_t, heads_t_far, sibling(me))
    loads[6].wait()

    def add(target, term):
        add_into(target, [term])

    total = RingSum(
        wire, me, "x", columns_of(out_part), out_near_left, out_near_right, out_whole_left,
        out_whole_right, add,
    ).start()
    loads[1].wait()

    def back_heads(zl, carry):
        weight = jnp.concatenate(
            [w_o[zl, y, zh, c] for y in range(4) for zh in range(2) for c in range(2)], axis=1
        )
        result = dot_nt(d_attn[...].reshape(512, D), weight).astype(BF)
        d_heads[zl * 2] = result[:, 0:HD]
        d_heads[zl * 2 + 1] = result[:, HD : 2 * HD]
        return carry

    lax.fori_loop(0, 2, back_heads, 0)
    fill_bias(bias, me, start_in[0])
    loads[7].wait()

    def grad_o(index, carry):
        zl, y = lax.div(index, 4), lax.rem(index, 4)
        mine = jnp.concatenate(
            [
                d_attn[:, :, pl.ds(pl.multiple_of(((y * 2 + zh) * 2 + me.core) * 128, 128), 128)]
                .reshape(512, 128)
                for zh in range(2)
            ],
            axis=1,
        )
        other = jnp.concatenate(
            [attn_far[y * 2 + zh].reshape(512, 128) for zh in range(2)], axis=1
        )
        rows = pl.ds(pl.multiple_of(zl * 256, 256), 256)
        result = (dot_nn(heads_t[rows, :], mine) + dot_nn(heads_t_far[rows, :], other)).astype(BF)
        g_o[zl, y, 0] = result[:, 0:128]
        g_o[zl, y, 1] = result[:, 128:256]
        return carry

    heads_put.wait_recv()
    for copy in attn_puts:
        copy.wait_recv()
    lax.fori_loop(0, 8, grad_o, 0)
    attn = [
        Fold(wire, me, fold_view(g_o, me, 0, "y", 0, 128, 64), ("y", "z"), bufs[4],
             crossed_view(g_o, me, 0, "z", 0, 128, 64), bufs[5]),
        Fold(wire, me, fold_view(g_o, me, 0, "z", 128, 128, 64), ("z", "y"), bufs[6],
             crossed_view(g_o, me, 0, "y", 128, 128, 64), bufs[7]),
    ]
    for item in attn:
        item.start()
    total.relay()
    for item in feed:
        item.relay_two()

    def back_attend(head, carry):
        for half, span in ((1, 1024), (0, 768)):
            rows = slice(half * 256, half * 256 + 256)
            key, value = keys_in[head, 0:span, :], values_in[head, 0:span, :]
            query, d_head = query_in[head, rows, :], d_heads[head, rows, :]
            scores = dot_nt(key, query) * SCALE + bias[0:span, rows]
            probs = jnp.exp(scores - lse_in[head, :, rows])
            d_probs = dot_nt(value, d_head)
            delta = jnp.sum(probs * d_probs, axis=0, keepdims=True)
            d_scores = (probs * (d_probs - delta) * SCALE).astype(BF)
            d_key = dot_nn(d_scores, query)
            d_value = dot_nn(probs.astype(BF), d_head)
            if half == 1:
                sum_keys[...] = d_key
                sum_values[...] = d_value
            else:
                sum_keys[0:span, :] += d_key
                sum_values[0:span, :] += d_value
            raw = dot_tn(key, d_scores).T
            cosine = tables[0, 2 * half : 2 * half + 2, 0].reshape(256, HD)
            sine = tables[1, 2 * half : 2 * half + 2, 0].reshape(256, HD)
            column = pl.ds(pl.multiple_of(head * HD, HD), HD)
            d_query[rows, column] = turn(raw, cosine, -sine).astype(BF)
        cosine, sine = tables[0].reshape(SEQ, HD), tables[1].reshape(SEQ, HD)
        d_keys[:, column] = turn(sum_keys[...], cosine, -sine).astype(BF)
        d_values[:, column] = sum_values[...].astype(BF)
        return carry

    lax.fori_loop(0, 2, back_attend, 0)
    for item in attn:
        item.relay()
    for item, out in zip(feed[:2], (g_wide_out.at[:, 0:64, :], g_wide_out.at[:, 64:128, :])):
        item.finish(out)
    for item, out in zip(feed[2:], (g_down_out.at[0:352, :], g_down_out.at[352:UNITS, :])):
        item.finish(out)
    lax.fori_loop(2, 4, back_attend, 0)
    grads_put = [
        wire.put(d_query, d_query_far, sibling(me)),
        wire.put(d_keys, d_keys_far, sibling(me)),
        wire.put(d_values, d_values_far, sibling(me)),
    ]
    for item in attn:
        item.turn()
    for copy in loads[8:]:
        copy.wait()

    def back_h(block, carry):
        y, zh = lax.div(block, 2), lax.rem(block, 2)

        def weight(which):
            return jnp.concatenate(
                [w_qkv[which, 0, y, zh].reshape(256, 256), w_qkv[which, 1, y, zh].reshape(256, 256)],
                axis=1,
            )

        column = pl.ds(pl.multiple_of(block * 256, 256), 256)
        both = dot_nt(d_keys[...], weight(1)) + dot_nt(d_values[...], weight(2))
        both = both.reshape(4, 2, 128, 256)
        own = dot_nt(d_query[...], weight(0)).reshape(4, 128, 256) + both[:, 0]
        d_h[:, 0, :, column] = own.astype(BF)
        d_h[:, 1, :, column] = both[:, 1].astype(BF)
        return carry

    lax.fori_loop(0, 8, back_h, 0)
    one, far, three = rem4(me.x + 1), rem4(me.x + 2), rem4(me.x + 3)
    to_z = wire.put(d_h.at[far, 1], far_one, partner(me))
    to_right = wire.put(d_h.at[one, 1], side_left, near(me, "x", 1))
    to_left = wire.put(d_h.at[three, 1], side_right, near(me, "x", 3))

    total.finish()

    def finish_out(index, carry):
        span = pl.ds(pl.multiple_of(index * 16, 16), 16)
        result_out[span, :] = (
            y_in[span, :]
            + (
                out_part[me.x, span, :].astype(F32)
                + out_whole_left[span, :].astype(F32)
                + out_whole_right[span, :].astype(F32)
            )
        ).astype(BF)
        return carry

    lax.fori_loop(0, 8, finish_out, 0)
    for copy in grads_put:
        copy.wait_recv()

    def blocks(which, pair):
        return turned[which, pl.ds(pair * 4, 4)].reshape(512, SEQ)

    def own_rows(value):
        return jnp.concatenate([value[:, i * 256 : i * 256 + 128] for i in range(4)], axis=1)

    def grad_qkv(index, carry):
        zl, pair = lax.div(index, 2), lax.rem(index, 2)
        column = pl.ds(pl.multiple_of(zl * 256, 256), 256)
        mine, other = blocks(0, pair), blocks(1, pair)
        result = dot_nn(own_rows(mine), d_query[:, column])
        result = result + dot_nn(own_rows(other), d_query_far[:, column])
        g_qkv[0, zl, pl.ds(pair * 2, 2)] = result.astype(BF).reshape(2, 2, 128, 256)
        result = dot_nn(mine, d_keys[:, column]) + dot_nn(other, d_keys_far[:, column])
        g_qkv[1, zl, pl.ds(pair * 2, 2)] = result.astype(BF).reshape(2, 2, 128, 256)
        result = dot_nn(mine, d_values[:, column]) + dot_nn(other, d_values_far[:, column])
        g_qkv[2, zl, pl.ds(pair * 2, 2)] = result.astype(BF).reshape(2, 2, 128, 256)
        return carry

    lax.fori_loop(0, 4, grad_qkv, 0)
    more = [
        Fold(wire, me, fold_view(g_qkv, me, 1, "y", 0, 64, 32), ("y", "z"), bufs[8],
             crossed_view(g_qkv, me, 1, "z", 0, 64, 32), bufs[9]),
        Fold(wire, me, fold_view(g_qkv, me, 1, "z", 64, 64, 32), ("z", "y"), bufs[10],
             crossed_view(g_qkv, me, 1, "y", 64, 64, 32), bufs[11]),
    ]
    for item in more:
        item.start()

    to_z.wait_recv()
    add_into(d_h.at[far, 0], [far_one])
    own_part = RingSum(
        wire, me, "x",
        lambda slot, half: d_h.at[slot, 0] if half is None else d_h.at[slot, 0, :, pl.ds(half * 1024, 1024)],
        near_left, near_right, whole_left, whole_right, add,
    ).start()
    to_right.wait_recv()
    to_left.wait_recv()
    add_into(d_h.at[me.x, 1], [side_left, side_right])
    to_z = wire.put(d_h.at[me.x, 1], last_z, partner(me))
    for item in attn:
        item.relay_two()
    own_part.relay()
    for item in more:
        item.relay()
    for item, out in zip(attn, (g_o_out.at[0:128, :], g_o_out.at[128:256, :])):
        item.finish(out)
    for item in more:
        item.turn()
    own_part.finish()
    to_z.wait_recv()

    gain_one = gains_in[0:1, :]

    def back_norm(index, carry):
        span = pl.ds(pl.multiple_of(index * 16, 16), 16)
        d_h_one = (
            d_h[me.x, 0, span, :].astype(F32)
            + whole_left[span, :].astype(F32)
            + whole_right[span, :].astype(F32)
            + last_z[span, :].astype(F32)
        )
        value = tok[span, :].astype(F32)
        scale = lax.rsqrt(jnp.mean(value * value, axis=-1, keepdims=True) + EPS)
        normed = value * scale
        e_one = d_h_one * gain_one
        inner = jnp.mean(e_one * normed, axis=-1, keepdims=True)
        tokens_out[span, :] = (dy_in[span, :] + scale * (e_one - normed * inner)).astype(BF)
        return carry + jnp.sum(d_h_one * normed, axis=0, keepdims=True)

    gain_t[0:1, :] = lax.fori_loop(0, 8, back_norm, jnp.zeros((1, D), F32))
    gain_t[1:2, :] = gain_in[...]
    for row in range(2):
        for block in range(16):
            gain_x[me.x, row * 16 + block : row * 16 + block + 1, :] = gain_t[
                row : row + 1, block * 128 : block * 128 + 128
            ]
    ring = Ring(wire, me, "x", lambda slot, half: gain_x.at[slot]).start()
    for item in more:
        item.relay_two()
    ring.relay(False).finish()
    gain_z[me.z] = gain_x[0] + gain_x[1] + gain_x[2] + gain_x[3]
    Ring(wire, me, "z", lambda slot, half: gain_z.at[slot]).start().relay(False).finish()
    gain_y[me.y] = gain_z[0] + gain_z[1] + gain_z[2] + gain_z[3]
    Ring(wire, me, "y", lambda slot, half: gain_y.at[slot]).start().relay(False).finish()
    gain_c[me.core] = gain_y[0] + gain_y[1] + gain_y[2] + gain_y[3]
    piece = gain_c.at[me.core]
    wire.put(piece, piece, sibling(me)).wait_recv()
    gains_out[...] = gain_c[0] + gain_c[1]
    for item, out in zip(more, (g_qkv_out.at[:, 0:64, :], g_qkv_out.at[:, 64:128, :])):
        item.finish(out)
    wire.drain()


def call_back(starts, tokens, d_attn, out_part, qkv, w_out, query, keys, values, heads, lse, turned,
              tables, gains, y_one, d_y, gain_two, wide_y, wide_z, down_y, down_z):
    shape = jax.ShapeDtypeStruct
    bufs = (
        fold_shapes((2,), (), 64, 32, UNITS)
        + fold_shapes((2,), (), 64, 32, UNITS)
        + fold_shapes((), (), 352, 176, 128)
        + fold_shapes((), (), 336, 176, 128)
        + fold_shapes((), (2, 2), 128, 64, 128)
        + fold_shapes((), (), 128, 64, 128)
        + fold_shapes((), (4,), 128, 64, 128)
        + fold_shapes((), (), 128, 64, 128)
        + fold_shapes((3,), (2, 2), 64, 32, 256)
        + fold_shapes((3,), (), 64, 32, 256)
        + fold_shapes((3,), (4,), 64, 32, 256)
        + fold_shapes((3,), (), 64, 32, 256)
    )
    return pl.pallas_call(
        kernel_back,
        name="back",
        in_specs=[pl.BlockSpec(memory_space=pltpu.SMEM)]
        + [anywhere()] * 5
        + [in_vmem()] * 5
        + [anywhere()] * 2
        + [in_vmem()] * 4
        + [anywhere()] * 4,
        out_specs=[in_vmem()] * 7,
        out_shape=[
            shape((128, D), BF),
            shape((128, D), BF),
            shape((3, 128, 256), F32),
            shape((256, 128), F32),
            shape((2, 128, UNITS), F32),
            shape((UNITS, 128), F32),
            shape((32, 128), F32),
        ],
        scratch_shapes=[
            pltpu.VMEM((3, 2, 4, 2, 2, 128, 256), BF),
            pltpu.VMEM((2, 4, 2, 2, 256, 128), BF),
            pltpu.VMEM((4, 128, D), BF),
            pltpu.VMEM((4, 128, D), BF),
            pltpu.VMEM((2, 4, 2, 128, HD), F32),
            pltpu.VMEM((SEQ, 512), F32),
            pltpu.VMEM((128, D), BF),
            pltpu.VMEM((2, 8, 128, SEQ), BF),
            pltpu.VMEM((4, 512, HD), BF),
            pltpu.VMEM((512, 512), BF),
            pltpu.VMEM((SEQ, 512), BF),
            pltpu.VMEM((SEQ, 512), BF),
            pltpu.VMEM((512, 512), BF),
            pltpu.VMEM((SEQ, 512), BF),
            pltpu.VMEM((SEQ, 512), BF),
            pltpu.VMEM((SEQ, HD), F32),
            pltpu.VMEM((SEQ, HD), F32),
            pltpu.VMEM((512, 512), BF),
            pltpu.VMEM((512, 512), BF),
            pltpu.VMEM((8, 4, 128, 128), BF),
            pltpu.VMEM((4, 2, 128, D), BF),
        ]
        + [pltpu.VMEM((128, D), BF)] * 4
        + [
            pltpu.VMEM((128, D // 2), BF),
            pltpu.VMEM((128, D // 2), BF),
            pltpu.VMEM((128, D), BF),
            pltpu.VMEM((128, D), BF),
        ]
        * 2
        + [
            pltpu.VMEM((3, 2, 4, 2, 128, 256), BF),
            pltpu.VMEM((2, 4, 2, 256, 128), BF),
            pltpu.VMEM((2, 2, 2, 64, UNITS), BF),
            pltpu.VMEM((2, 4, 64, UNITS), BF),
            pltpu.VMEM((2, 2, 352, 128), BF),
            pltpu.VMEM((4, 336, 128), BF),
            pltpu.VMEM((2, D), F32),
            pltpu.VMEM((4, 32, 128), F32),
            pltpu.VMEM((4, 32, 128), F32),
            pltpu.VMEM((4, 32, 128), F32),
            pltpu.VMEM((2, 32, 128), F32),
        ]
        + bufs
        + [
            pltpu.SemaphoreType.DMA((90,)),
            pltpu.SemaphoreType.DMA((90,)),
            pltpu.SemaphoreType.DMA((16,)),
        ],
        compiler_params=pltpu.CompilerParams(
            collective_id=2, has_side_effects=True, vmem_limit_bytes=VMEM_BYTES
        ),
    )(starts, tokens, d_attn, out_part, qkv, w_out, query, keys, values, heads, lse, turned,
      tables, gains, y_one, d_y, gain_two, wide_y, wide_z, down_y, down_z)


def on_device(tables, tokens, starts, w_query, w_key, w_value, w_out, w_gate, w_up, w_down,
              gain_attn, gain_mlp, cotangent):
    qkv = jnp.stack([w_query, w_key, w_value])
    wide = jnp.stack([w_gate, w_up])
    tile = gain_tile(gain_attn, gain_mlp)
    (qkv, w_o, wide, down, cot, turned, query, keys, values, heads, lse, y_one, h_two, gains) = (
        call_attend(tokens, cotangent, starts, qkv, w_out, wide, w_down, tile, tables)
    )
    (out_part, d_attn, wide_y, wide_z, down_y, down_z, d_y, gain_two) = call_feed(
        h_two, cot, wide, down, y_one, gains
    )
    result, grad_tokens, g_qkv, g_o, g_wide, g_down, g_gains = call_back(
        starts, tokens, d_attn, out_part, qkv, w_o, query, keys, values, heads, lse, turned,
        tables, gains, y_one, d_y, gain_two, wide_y, wide_z, down_y, down_z,
    )
    dp, tp = lax.axis_index("dp"), lax.axis_index("tensor")
    grad_attn = lax.dynamic_slice(g_gains, (dp, tp * 16), (1, 16))[0]
    grad_mlp = lax.dynamic_slice(g_gains, (16 + dp, tp * 16), (1, 16))[0]
    return (
        result, grad_tokens, g_qkv[0], g_qkv[1], g_qkv[2], g_o, g_wide[0], g_wide[1], g_down,
        grad_attn, grad_mlp,
    )


def solution(mesh):
    both = ("dp", "tensor")
    rows, wide, tall = P(both, None), P("dp", "tensor"), P("tensor", "dp")
    in_specs = (
        rows, P("dp"), wide, wide, wide, tall, wide, wide, tall, P(both), P(both), rows,
    )
    out_specs = (
        rows, rows, wide, wide, wide, tall, wide, wide, tall, P(both), P(both),
    )
    return jax.shard_map(
        functools.partial(on_device, rope_tables()), mesh=mesh, in_specs=in_specs,
        out_specs=out_specs, check_vma=False,
    )
```

time: 1690 us -> 367 us (0.22)
  waiting for transfers between devices: 1260 us -> 0 us
  Pallas kernels: 0 us -> 352 us
  matrix products: 165 us -> 0 us
  blocking collectives: 150 us -> 0 us
  other arithmetic: 40.8 us -> 3.07 us
  local copies, waits for them, and re-layouts: 42.3 us -> 10.5 us
    all_gather x11 -> x0, waiting for transfers between devices: 568 us -> none  [the longest x4 317 us: spread_rows(): return lax.all_gather(piece, 'tensor', axis=0, tiled=True)]
    reduce_scatter x7 -> x0, waiting for transfers between devices: 490 us -> none  [the longest x4 285 us: sum_rows(): lax.psum_scatter(partial_sum.astype(jnp.bfloat16), 'tensor', scatter_dime...]
    pallas_call x0 -> x3, Pallas kernels: none -> 352 us  [the longest x1 154 us: call_attend(): pl.pallas_call(kernel_attend, name='attend', in_specs=[anywhere(), anywhe...]
    unnamed x26 -> x0, waiting for transfers between devices: 201 us -> none
    dot_general x35 -> x0, matrix products: 165 us -> none  [the longest x7 40.1 us: dot_rows(): lax.dot_general(left, right, (((0,), (0,)), ((), ())), preferred_element_...]
    unnamed x2 -> x0, blocking collectives: 150 us -> none
    unnamed x73 -> x20, local copies, waits for them, and re-layouts: 31.6 us -> 6.91 us
    convert_element_type x13 -> x0, other arithmetic: 16.9 us -> none  [the longest x4 5.18 us: on_device(): grad_query, grad_key, grad_value, grad_out = (lax.psum_scatter(grad_query...]
  transfers between devices with their start and end apart: 22 -> 0, of which waited for: 20 -> 0; matrix products, arithmetic and copies ran while one was open for 12% -> 0% of each run, Pallas kernels for 0% -> 0%
where the time goes in v1:
time: 367 us
  Pallas kernels  352 us (96%)
  local copies, waits for them, and re-layouts  10.5 us (3%)
    pallas_call x1, Pallas kernels, call_attend(): pl.pallas_call(kernel_attend, name='attend', in_specs=[anywhere(), anywhe...  154 us
    pallas_call x1, Pallas kernels, call_feed(): pl.pallas_call(kernel_feed, name='feed', in_specs=[anywhere()] * 4 + [in_...  99.1 us
    pallas_call x1, Pallas kernels, call_back(): pl.pallas_call(kernel_back, name='back', in_specs=[pl.BlockSpec(memory_sp...  98.6 us

profile of v1, /device:TPU:1, one launch (start us, length us, event | category | flops | bytes accessed | tf_op | source)
XLA Modules:
  0.0 366.9 jit_solution(6787602667335038017)
XLA Ops:
  0.6 0.7 pad_maximum_fusion.2
  1.3 0.3 dynamic_update_slice.3.tile_in
  1.7 0.0 copy-start.5
  2.3 1.1 copy.24
  3.4 1.1 copy.25
  4.4 0.8 pad_maximum_fusion.wide_in
  5.2 1.6 pad_maximum_fusion.1.qkv_in
  6.8 0.0 copy-done.5
  6.8 154.2 %attend.1 = (bf16[3,2,4,2,2,128,256]{6,5,4,3,2,1,0:T(8,128)(2,1)}, bf16[2,4,2,2,256,128]{5,4,3,2,1,0:T(8,128)(2,1)}, bf16[2,2,4,2,2,128,688]{6,5,4,3,2,1,0:T(8,1...) custom-call(bf16[128,2048]{1,0:T(8,128)(2,1)} %tokens_in.3, ...), custom_call_target="tpu_custom_call" | custom-call | tf_op jit(solution)/shard_map/attend/pallas_call | solution.py:500
  161.0 99.1 %feed.1 = (bf16[4,128,2048]{2,1,0:T(8,128)(2,1)}, bf16[4,128,2048]{2,1,0:T(8,128)(2,1)}, bf16[2,2,2,64,688]{4,3,2,1,0:T(8,128)(2,1)}, bf16[2,4,64,688]{3,2,1,0:T...) custom-call(bf16[128,2048]{1,0:T(8,128)(2,1)} %get-tuple-element.40., ...), custom_call_target="tpu_custom_call" | custom-call | tf_op jit(solution)/shard_map/feed/pallas_call | solution.py:839
  260.1 98.6 %back.1 = (bf16[128,2048]{1,0:T(8,128)(2,1)}, bf16[128,2048]{1,0:T(8,128)(2,1)}, f32[3,128,256]{2,1,0:T(8,128)}, f32[256,128]{1,0:T(8,128)}, f32[2,128,688]{2,1,...) custom-call(s32[1]{0:T(128)S(6)} %copy.33.start_in, bf16[128,2048]{1,0:T(8,128)(2,1)} %tokens_in.3, ...), custom_call_target="tpu_custom_call" | custom-call | tf_op jit(solution)/shard_map/back/pallas_call | solution.py:1280
  358.7 0.0 copy-start.2
  358.7 0.0 copy-start.1
  358.7 0.0 copy-start
  358.8 1.3 slice_bitcast_fusion
  360.0 0.0 copy-start.4
  360.0 0.9 copy.26
  360.9 0.0 copy-start.3
  360.9 0.9 copy.27
  361.8 0.0 copy-done.2
  361.9 0.8 slice_bitcast_fusion.2
  362.6 1.3 dynamic-slice_bitcast_fusion
  363.9 0.0 copy-done.1
  363.9 0.8 copy.34
  364.7 0.0 copy-done
  364.7 0.8 copy.35
  365.5 0.0 copy-done.4
  365.5 0.7 copy.36
  366.1 0.0 copy-done.3
  366.1 0.7 copy.37
  (1 shorter events, 0.0 us)
Async XLA Ops:
  1.7 5.2 %copy-start.5 = (f32[8,128]{1,0:T(8,128)}, f32[8,128]{1,0:T(8,128)S(1)}, u32[]{:S(2)}) copy-start(f32[8,128]{1,0:T(8,128)S(1)} %dynamic_update_slice.3.tile_in) | copy-start | bytes 12292
  358.7 3.1 copy-start.2
  358.7 5.1 %copy-start.1 = (bf16[128,2048]{1,0:T(8,128)(2,1)S(1)}, bf16[128,2048]{1,0:T(8,128)(2,1)}, u32[]{:S(2)}) copy-start(bf16[128,2048]{1,0:T(8,128)(2,1)} %get-tuple-element.98) | copy-start | bytes 1572868
  358.7 5.9 %copy-start = (bf16[128,2048]{1,0:T(8,128)(2,1)S(1)}, bf16[128,2048]{1,0:T(8,128)(2,1)}, u32[]{:S(2)}) copy-start(bf16[128,2048]{1,0:T(8,128)(2,1)} %get-tuple-element.99) | copy-start | bytes 1572868
  360.0 5.4 %copy-start.4 = (f32[256,128]{1,0:T(8,128)S(1)}, f32[256,128]{1,0:T(8,128)}, u32[]{:S(2)}) copy-start(f32[256,128]{1,0:T(8,128)} %get-tuple-element.103) | copy-start | bytes 393220
  360.9 5.2 %copy-start.3 = (f32[688,128]{1,0:T(8,128)S(1)}, f32[688,128]{1,0:T(8,128)}, u32[]{:S(2)}) copy-start(f32[688,128]{1,0:T(8,128)} %get-tuple-element.106) | copy-start | bytes 1056772

commit v2 on v1

v2 whole, which is shorter than its diff:
```python
import functools
import math
import types

import jax
import jax.numpy as jnp
import numpy as np
from jax import lax
from jax.experimental import pallas as pl
from jax.experimental.pallas import tpu as pltpu
from jax.sharding import PartitionSpec as P

HD = 128
PIECE = 256
EPS = 1e-05
NEG = -1e30
SCALE = HD ** (-0.5)
D = 2048
SEQ = 1024
UNITS = 688
BF = jnp.bfloat16
F32 = jnp.float32
MESH = pl.DeviceIdType.MESH
VMEM_BYTES = 60 * 1024 * 1024
ALL = slice(None)


def dot_nn(left, right):
    return jnp.dot(left, right, preferred_element_type=F32)


def dot_nt(left, right):
    return lax.dot_general(left, right, (((1,), (1,)), ((), ())), preferred_element_type=F32)


def dot_tn(left, right):
    return lax.dot_general(left, right, (((0,), (0,)), ((), ())), preferred_element_type=F32)


def rem4(value):
    return lax.rem(value, 4)


def place():
    dp = lax.axis_index("dp")
    tp = lax.axis_index("tensor")
    zh = lax.rem(lax.div(dp, 2), 2)
    zl = lax.rem(tp, 2)
    return types.SimpleNamespace(
        y=lax.div(dp, 4), zh=zh, zl=zl, z=zh * 2 + zl, x=lax.div(tp, 2), core=lax.rem(dp, 2)
    )


def device(me, **moved):
    at = types.SimpleNamespace(**{**vars(me), **moved})
    zh, zl = lax.div(at.z, 2), lax.rem(at.z, 2)
    return (at.y * 4 + zh * 2 + at.core, at.x * 2 + zl)


def near(me, axis, step):
    return device(me, **{axis: rem4(getattr(me, axis) + step)})


def sibling(me):
    return device(me, core=1 - me.core)


def partner(me):
    return device(me, z=me.zh * 2 + 1 - me.zl)


def greet(me, wide):
    others = [near(me, axis, step) for axis in ("x", "y", "z") for step in (1, 3)] + [sibling(me)]
    if wide:
        others += [near(me, axis, 2) for axis in ("x", "y", "z")]
        others += [crossed(me, step) for step in (1, 2, 3)]
    barrier = pltpu.get_barrier_semaphore()
    for other in others:
        pl.semaphore_signal(barrier, inc=1, device_id=other, device_id_type=MESH)
    pl.semaphore_wait(barrier, len(others))


def crossed(me, step):
    return device(me, y=rem4(me.y + step), core=1 - me.core)


class Wire:
    def __init__(self, send, recv, local):
        self.send, self.recv, self.local = send, recv, local
        self.used, self.used_local = 0, 0
        self.sent = []

    def put(self, source, target, to):
        index = self.used
        self.used += 1
        copy = pltpu.make_async_remote_copy(
            src_ref=source,
            dst_ref=target,
            send_sem=self.send.at[index],
            recv_sem=self.recv.at[index],
            device_id=to,
            device_id_type=MESH,
        )
        copy.start()
        self.sent.append(copy)
        return copy

    def move(self, source, target):
        index = self.used_local
        self.used_local += 1
        copy = pltpu.make_async_copy(source, target, self.local.at[index])
        copy.start()
        return copy

    def settle(self, copies):
        for copy in copies:
            copy.wait_send()
        done = {id(copy) for copy in copies}
        self.sent = [copy for copy in self.sent if id(copy) not in done]

    def drain(self):
        for copy in self.sent:
            copy.wait_send()
        self.sent = []


class Ring:
    def __init__(self, wire, me, axis, view):
        self.wire, self.view = wire, view
        self.at = getattr(me, axis)
        self.right, self.left = near(me, axis, 1), near(me, axis, 3)

    def put(self, slot, part, to):
        piece = self.view(slot, part)
        return self.wire.put(piece, piece, to)

    def start(self):
        self.right_one = self.put(self.at, 0, self.right)
        self.left_one = self.put(self.at, 1, self.left)
        self.right_two = self.put(self.at, 1, self.right)
        self.left_two = self.put(self.at, 0, self.left)
        return self

    def relay(self):
        self.right_one.wait_recv()
        self.far_right = self.put(rem4(self.at + 3), 0, self.right)
        self.left_one.wait_recv()
        self.far_left = self.put(rem4(self.at + 1), 1, self.left)
        return self

    def close(self):
        self.right_two.wait_recv()
        self.left_two.wait_recv()
        return self

    def finish(self):
        self.far_right.wait_recv()
        self.far_left.wait_recv()
        return self


class Meet:
    def __init__(self, wire, me, axis, ref):
        piece = ref.at[getattr(me, axis)]
        self.copies = [wire.put(piece, piece, near(me, axis, step)) for step in (1, 2, 3)]

    def finish(self):
        for copy in self.copies:
            copy.wait_recv()


class MeetCores:
    def __init__(self, wire, me, ref):
        piece = ref.at[me.core, me.y]
        others = [near(me, "y", step) for step in (1, 2, 3)] + [sibling(me)]
        others += [crossed(me, step) for step in (1, 2, 3)]
        self.copies = [wire.put(piece, piece, other) for other in others]

    finish = Meet.finish


class RingSum:
    def __init__(self, wire, me, axis, part, from_left, from_right, whole_left, whole_right, split, add):
        self.wire, self.part, self.split, self.add = wire, part, split, add
        self.at = getattr(me, axis)
        self.right, self.left = near(me, axis, 1), near(me, axis, 3)
        self.near_bufs = (from_left, from_right)
        self.whole = (whole_left, whole_right)

    def start(self, halves=(0, 1)):
        after, far, before = rem4(self.at + 1), rem4(self.at + 2), rem4(self.at + 3)
        put, part, split = self.wire.put, self.part, self.split
        if 0 in halves:
            self.first = put(part(far, 0), self.near_bufs[0], self.right)
        if 1 in halves:
            self.second = put(part(far, 1), self.near_bufs[1], self.left)
        if 0 in halves:
            self.left_whole = put(part(before, 0), split(self.whole[1], 0), self.left)
        if 1 in halves:
            self.right_whole = put(part(after, 1), split(self.whole[0], 1), self.right)
        return self

    def relay(self):
        after, before = rem4(self.at + 1), rem4(self.at + 3)
        self.first.wait_recv()
        self.add(self.part(after, 0), self.near_bufs[0])
        self.to_right = self.wire.put(self.part(after, 0), self.split(self.whole[0], 0), self.right)
        self.second.wait_recv()
        self.add(self.part(before, 1), self.near_bufs[1])
        self.to_left = self.wire.put(self.part(before, 1), self.split(self.whole[1], 1), self.left)
        return self

    def finish(self):
        for copy in (self.left_whole, self.right_whole, self.to_right, self.to_left):
            copy.wait_recv()
        return self


def split_columns(ref, half):
    return ref.at[:, pl.ds(half * (D // 2), D // 2)]


def split_rows(cut):
    def split(ref, half):
        rows = ref.shape[-2]
        span = pl.ds(0, cut) if half == 0 else pl.ds(cut, rows - cut)
        return ref.at[(ALL,) * (len(ref.shape) - 2) + (span, ALL)]

    return split


class Spread:
    def __init__(self, wire, me, ref, lead, row, rows, first, cut):
        self.wire, self.me = wire, me
        head = (ALL,) * lead

        def view(y, z, part):
            zl, zh = (ALL, ALL) if z is None else (lax.rem(z, 2), lax.div(z, 2))
            start, size = row, rows
            if part == 0:
                size = cut
            if part == 1:
                start, size = row + cut, rows - cut
            yy = ALL if y is None else y
            return ref.at[head + (zl, yy, zh, me.core, pl.ds(start, size), ALL)]

        self.view = view
        if first == "y":
            self.one = Ring(wire, me, "y", lambda slot, part: view(slot, me.z, part))
            self.two = Ring(wire, me, "z", lambda slot, part: view(None, slot, part))
        else:
            self.one = Ring(wire, me, "z", lambda slot, part: view(me.y, slot, part))
            self.two = Ring(wire, me, "y", lambda slot, part: view(slot, None, part))
        self.shared = []

    def share(self, slot):
        piece = self.two.view(slot, None)
        self.shared.append(self.wire.put(piece, piece, sibling(self.me)))

    def turn(self):
        self.one.close().finish()
        self.two.start()
        self.share(self.two.at)

    def relay(self):
        self.two.relay()

    def finish(self):
        self.two.close()
        self.share(rem4(self.two.at + 3))
        self.share(rem4(self.two.at + 1))
        self.two.finish()
        self.share(rem4(self.two.at + 2))

    def wait(self):
        for copy in self.shared:
            copy.wait_recv()


def norm_rows(source, target, gain, rows, step=32):
    def body(index, carry):
        span = pl.ds(pl.multiple_of(index * step, step), step)
        value = source[span, :].astype(F32)
        scale = lax.rsqrt(jnp.mean(value * value, axis=-1, keepdims=True) + EPS)
        target[span, :] = (value * scale * gain).astype(BF)
        return carry

    lax.fori_loop(0, rows // step, body, 0)


def fill_bias(bias, me, start):
    row = lax.broadcasted_iota(jnp.int32, (128, 512), 0)
    column = lax.broadcasted_iota(jnp.int32, (128, 512), 1)
    query = lax.div(column, 128) * 256 + me.zl * 128 + lax.rem(column, 128)
    query_in = (query >= start) & (query < start + PIECE)

    def body(block, carry):
        pair, other = lax.div(block, 2), lax.rem(block, 2)
        parity = me.zl + other * (1 - 2 * me.zl)
        key = (pair * 2 + parity) * 128 + row
        key_in = (key >= start) & (key < start + PIECE)
        allowed = (key <= query) | (query_in & key_in)
        bias[pl.ds(pl.multiple_of(block * 128, 128), 128), :] = jnp.where(allowed, 0.0, NEG)
        return carry

    lax.fori_loop(0, 8, body, 0)


def turn(field, cosine, sine):
    return field * cosine + pltpu.roll(field, HD // 2, 1) * sine


def add_into(target, terms, result=None):
    shape = target.shape
    lead, rows, columns = shape[:-2], shape[-2], shape[-1]
    step = rows
    while step * columns > 33000:
        step = next(s for s in range(step - 16, 0, -16) if rows % s == 0)
    cuts = rows // step
    result = target if result is None else result

    def body(index, carry):
        where, rest = [], lax.div(index, cuts)
        for extent in reversed(lead):
            where.insert(0, lax.rem(rest, extent))
            rest = lax.div(rest, extent)
        where = tuple(where) + (
            pl.ds(pl.multiple_of(lax.rem(index, cuts) * step, 16), step), ALL
        )
        total = target[where].astype(F32)
        for term in terms:
            total = total + term[where].astype(F32)
        result[where] = total.astype(result.dtype)
        return carry

    lax.fori_loop(0, math.prod(lead) * cuts, body, 0)


def columns_of(ref):
    def view(slot, half):
        if half is None:
            return ref.at[slot]
        return ref.at[slot, :, pl.ds(half * (D // 2), D // 2)]

    return view


def rows_of(ref):
    def view(slot, half):
        return ref.at[slot] if half is None else ref.at[slot, pl.ds(half * 64, 64)]

    return view


def kernel_attend(
    tokens_in, cotangent_in, start_in, query_w, key_w, value_w, out_w, gate_w, up_w, down_w,
    gain_one_in, gain_two_in, tables_in,
    qkv_out, wo_out, mlp_out, cot_out, turned_out, query_out, keys_out, values_out, heads_out,
    h_out, lse_out, y_out, gains_out,
    tok, h_one, w_qkv, w_o, w_mlp, tables, bias, query, keys, values, heads, cot, h_two,
    part, near_left, near_right, whole_left, whole_right,
    turned, gain_x, gain_z, gain_c,
    send, recv, local,
):
    me = place()
    wire = Wire(send, recv, local)
    own = [wire.move(tokens_in, tok.at[me.x, 0])]
    for index, ref in enumerate((query_w, key_w, value_w)):
        own.append(wire.move(ref, w_qkv.at[index, me.zl, me.y, me.zh, me.core]))
    own.append(wire.move(out_w, w_o.at[me.zl, me.y, me.zh, me.core]))
    for index, ref in enumerate((gate_w, up_w, down_w)):
        own.append(wire.move(ref, w_mlp.at[index, me.zl, me.y, me.zh, me.core]))
    own.append(wire.move(tables_in.at[me.zl], tables))
    own.append(wire.move(cotangent_in, cot.at[me.x]))
    lane = lax.div(lax.broadcasted_iota(jnp.int32, (1, 128), 1), 16)
    tensor = me.x * 2 + me.zl
    gain_x[me.x] = jnp.concatenate(
        [
            jnp.where(lane == tensor, jnp.concatenate([ref[...]] * 8, axis=1), 0.0)
            for ref in (gain_one_in, gain_two_in)
        ]
        + [jnp.zeros((6, 128), F32)],
        axis=0,
    )
    greet(me, True)
    one, far, three = rem4(me.x + 1), rem4(me.x + 2), rem4(me.x + 3)
    meet = Meet(wire, me, "x", gain_x)

    own[0].wait()
    rows_x = Ring(
        wire, me, "x",
        lambda slot, half: tok.at[slot, 0] if half is None else tok.at[slot, 0, pl.ds(half * 64, 64)],
    ).start()
    rows_z = wire.put(tok.at[me.x, 0], tok.at[me.x, 1], partner(me))
    for copy in own[1:5]:
        copy.wait()
    qkv = [
        Spread(wire, me, w_qkv, 1, 0, 64, "y", 32),
        Spread(wire, me, w_qkv, 1, 64, 64, "z", 32),
    ]
    outs = [
        Spread(wire, me, w_o, 0, 0, 128, "y", 64),
        Spread(wire, me, w_o, 0, 128, 128, "z", 64),
    ]
    mlp = [
        Spread(wire, me, w_mlp, 1, 0, 352, "y", 176),
        Spread(wire, me, w_mlp, 1, 352, 336, "z", 176),
    ]
    for item in qkv + outs:
        item.one.start()
    meet.finish()
    gain_z[me.z] = gain_x[0] + gain_x[1] + gain_x[2] + gain_x[3]
    meet = Meet(wire, me, "z", gain_z)
    for item in qkv + outs:
        item.one.relay()
    meet.finish()
    gain_c[me.core, me.y, 0] = gain_z[0] + gain_z[1]
    gain_c[me.core, me.y, 1] = gain_z[2] + gain_z[3]
    meet = MeetCores(wire, me, gain_c)
    for item in qkv:
        item.turn()
    for copy in own[5:]:
        copy.wait()
    fill_bias(bias, me, start_in[0])
    meet.finish()
    for y in range(4):
        for zh in range(2):
            for core in range(2):
                column = (y * 4 + zh * 2 + core) * 128
                gains_out[:, column : column + 128] = gain_c[core, y, zh]
    rows_x.relay()
    rows_z.wait_recv()
    other_right = wire.put(tok.at[me.x, 1], tok.at[me.x, 1], near(me, "x", 1))
    other_left = wire.put(tok.at[me.x, 1], tok.at[me.x, 1], near(me, "x", 3))
    gain_one, gain_two = gains_out[0:1, :], gains_out[1:2, :]

    norm_rows(tok.at[me.x, 0], h_one.at[me.x, 0], gain_one, 128)
    norm_rows(tok.at[me.x, 1], h_one.at[me.x, 1], gain_one, 128)
    rows_x.close()
    norm_rows(tok.at[one, 0], h_one.at[one, 0], gain_one, 128)
    norm_rows(tok.at[three, 0], h_one.at[three, 0], gain_one, 128)
    for item in qkv:
        item.relay()
    for item in outs:
        item.turn()
    for item in mlp:
        item.one.start()
    rows_x.finish()
    far_z = wire.put(tok.at[far, 0], tok.at[far, 1], partner(me))
    norm_rows(tok.at[far, 0], h_one.at[far, 0], gain_one, 128)
    for item in qkv:
        item.finish()
    for item in outs:
        item.relay()
    for item in mlp:
        item.one.relay()
    for item in qkv:
        item.wait()
    kept = [wire.move(w_qkv, qkv_out)]

    def project(zl, carry):
        rows = h_one[:, 0].reshape(512, D)
        cosine, sine = tables[0, :, 0].reshape(512, HD), tables[1, :, 0].reshape(512, HD)
        raw = dot_nn(rows, w_qkv[0, zl].reshape(D, 256))
        for j in range(2):
            query[zl * 2 + j] = turn(raw[:, j * HD : (j + 1) * HD], cosine, sine).astype(BF)
        raw = dot_nn(rows, w_qkv[1, zl].reshape(D, 256))
        for j in range(2):
            keys[zl * 2 + j, :, 0] = (
                turn(raw[:, j * HD : (j + 1) * HD], cosine, sine).astype(BF).reshape(4, 128, HD)
            )
        raw = dot_nn(rows, w_qkv[2, zl].reshape(D, 256))
        for j in range(2):
            values[zl * 2 + j, :, 0] = raw[:, j * HD : (j + 1) * HD].astype(BF).reshape(4, 128, HD)
        return carry

    lax.fori_loop(0, 2, project, 0)
    kept.append(wire.move(query, query_out))
    other_right.wait_recv()
    other_left.wait_recv()
    norm_rows(tok.at[one, 1], h_one.at[one, 1], gain_one, 128)
    norm_rows(tok.at[three, 1], h_one.at[three, 1], gain_one, 128)
    far_z.wait_recv()
    cot_x = Ring(wire, me, "x", rows_of(cot)).start()
    norm_rows(tok.at[far, 1], h_one.at[far, 1], gain_one, 128)

    def project_other(zl, carry):
        rows = h_one[:, 1].reshape(512, D)
        cosine, sine = tables[0, :, 1].reshape(512, HD), tables[1, :, 1].reshape(512, HD)
        raw = dot_nn(rows, w_qkv[1, zl].reshape(D, 256))
        for j in range(2):
            keys[zl * 2 + j, :, 1] = (
                turn(raw[:, j * HD : (j + 1) * HD], cosine, sine).astype(BF).reshape(4, 128, HD)
            )
        raw = dot_nn(rows, w_qkv[2, zl].reshape(D, 256))
        for j in range(2):
            values[zl * 2 + j, :, 1] = raw[:, j * HD : (j + 1) * HD].astype(BF).reshape(4, 128, HD)
        return carry

    lax.fori_loop(0, 2, project_other, 0)
    kept += [wire.move(keys, keys_out), wire.move(values, values_out)]
    for item in outs:
        item.finish()
    for item in mlp:
        item.turn()

    def attend(head, carry):
        for half, pairs in ((0, 3), (1, 4)):
            span = pairs * 256
            rows = slice(half * 256, half * 256 + 256)
            scores = dot_nt(keys[head, 0:pairs].reshape(span, HD), query[head, rows, :]) * SCALE
            scores = scores + bias[0:span, rows]
            top = jnp.max(scores, axis=0, keepdims=True)
            expo = jnp.exp(scores - top)
            total = jnp.sum(expo, axis=0, keepdims=True)
            probs = (expo * (1.0 / total)).astype(BF)
            result = dot_tn(values[head, 0:pairs].reshape(span, HD), probs)
            heads[rows, pl.ds(pl.multiple_of(head * HD, HD), HD)] = result.T.astype(BF)
            lse_out[head, :, rows] = top + jnp.log(total)
        return carry

    lax.fori_loop(0, 4, attend, 0)
    kept.append(wire.move(heads, heads_out))
    for item in outs:
        item.wait()
    kept.append(wire.move(w_o, wo_out))

    def project_out(block, carry):
        y, zh = lax.div(block, 2), lax.rem(block, 2)
        weight = jnp.concatenate(
            [
                jnp.concatenate([w_o[zl, y, zh, 0], w_o[zl, y, zh, 1]], axis=1)
                for zl in range(2)
            ],
            axis=0,
        )
        result = dot_nn(heads[...], weight).astype(BF).reshape(4, 128, 256)
        part[:, :, pl.ds(pl.multiple_of(block * 256, 256), 256)] = result
        return carry

    total = RingSum(
        wire, me, "x", columns_of(part), near_left, near_right, whole_left, whole_right,
        split_columns, lambda target, term: add_into(target, [term]),
    )
    lax.fori_loop(0, 4, project_out, 0)
    total.start((0,))
    lax.fori_loop(4, 8, project_out, 0)
    total.start((1,))
    cot_x.relay()

    def flip(block, carry):
        column = pl.ds(pl.multiple_of(block * 128, 128), 128)
        rows = h_one[:, :, :, column].reshape(SEQ, 128)
        turned[lax.rem(block, 2), lax.div(block, 2)] = rows.T
        return carry

    lax.fori_loop(0, 8, flip, 0)
    total.relay()
    for item in mlp:
        item.relay()
    lax.fori_loop(8, 16, flip, 0)
    kept.append(wire.move(turned.at[me.core], turned_out.at[0]))
    turned_far = wire.put(turned.at[1 - me.core], turned_out.at[1], sibling(me))
    cot_x.close().finish()
    kept.append(wire.move(cot, cot_out))
    total.finish()

    def finish(index, carry):
        span = pl.ds(pl.multiple_of(index * 32, 32), 32)
        value = tok[me.x, 0, span, :].astype(F32) + (
            part[me.x, span, :].astype(F32)
            + whole_left[span, :].astype(F32)
            + whole_right[span, :].astype(F32)
        )
        scale = lax.rsqrt(jnp.mean(value * value, axis=-1, keepdims=True) + EPS)
        y_out[span, :] = value
        h_two[me.x, span, :] = (value * scale * gain_two).astype(BF)
        return carry

    lax.fori_loop(0, 4, finish, 0)
    h_ring = Ring(wire, me, "x", rows_of(h_two)).start()
    for item in mlp:
        item.finish()
    for item, rows in zip(mlp, (pl.ds(0, 352), pl.ds(352, 336))):
        item.wait()
        kept.append(wire.move(w_mlp.at[:, :, :, :, :, rows], mlp_out.at[:, :, :, :, :, rows]))
    h_ring.relay()
    turned_far.wait_recv()
    h_ring.close().finish()
    kept.append(wire.move(h_two, h_out))
    for copy in kept:
        copy.wait()
    wire.drain()


def anywhere():
    return pl.BlockSpec(memory_space=pl.ANY)


def in_vmem():
    return pl.BlockSpec(memory_space=pltpu.VMEM)


def call_attend(tokens, cotangent, starts, weights, gain_attn, gain_mlp, tables):
    shape = jax.ShapeDtypeStruct
    hbm = [
        shape((3, 2, 4, 2, 2, 128, 256), BF),
        shape((2, 4, 2, 2, 256, 128), BF),
        shape((3, 2, 4, 2, 2, UNITS, 128), BF),
        shape((4, 128, D), BF),
        shape((2, 8, 128, SEQ), BF),
        shape((4, 512, HD), BF),
        shape((4, 4, 2, 128, HD), BF),
        shape((4, 4, 2, 128, HD), BF),
        shape((512, 512), BF),
        shape((4, 128, D), BF),
    ]
    vmem = [shape((4, 1, 512), F32), shape((128, D), F32), shape((8, D), F32)]
    return pl.pallas_call(
        kernel_attend,
        name="attend",
        in_specs=[anywhere(), anywhere(), pl.BlockSpec(memory_space=pltpu.SMEM)]
        + [anywhere()] * 7
        + [in_vmem()] * 2
        + [anywhere()],
        out_specs=[anywhere()] * len(hbm) + [in_vmem()] * len(vmem),
        out_shape=hbm + vmem,
        scratch_shapes=[
            pltpu.VMEM((4, 2, 128, D), BF),
            pltpu.VMEM((4, 2, 128, D), BF),
            pltpu.VMEM((3, 2, 4, 2, 2, 128, 256), BF),
            pltpu.VMEM((2, 4, 2, 2, 256, 128), BF),
            pltpu.VMEM((3, 2, 4, 2, 2, UNITS, 128), BF),
            pltpu.VMEM((2, 4, 2, 128, HD), F32),
            pltpu.VMEM((SEQ, 512), F32),
            pltpu.VMEM((4, 512, HD), BF),
            pltpu.VMEM((4, 4, 2, 128, HD), BF),
            pltpu.VMEM((4, 4, 2, 128, HD), BF),
            pltpu.VMEM((512, 512), BF),
            pltpu.VMEM((4, 128, D), BF),
            pltpu.VMEM((4, 128, D), BF),
            pltpu.VMEM((4, 128, D), BF),
            pltpu.VMEM((128, D // 2), BF),
            pltpu.VMEM((128, D // 2), BF),
            pltpu.VMEM((128, D), BF),
            pltpu.VMEM((128, D), BF),
            pltpu.VMEM((2, 8, 128, SEQ), BF),
            pltpu.VMEM((4, 8, 128), F32),
            pltpu.VMEM((4, 8, 128), F32),
            pltpu.VMEM((2, 4, 2, 8, 128), F32),
            pltpu.SemaphoreType.DMA((140,)),
            pltpu.SemaphoreType.DMA((140,)),
            pltpu.SemaphoreType.DMA((24,)),
        ],
        compiler_params=pltpu.CompilerParams(
            collective_id=0, has_side_effects=True, vmem_limit_bytes=VMEM_BYTES
        ),
    )(tokens, cotangent, starts, *weights, gain_attn, gain_mlp, tables)


def rope_tables():
    half = HD // 2
    freq = np.exp(np.arange(half, dtype=np.float32) * np.float32(-2.0 * math.log(10000.0) / HD))
    order = np.array(
        [
            [[(2 * pair + (zl + other) % 2) * 128 + np.arange(128) for other in range(2)] for pair in range(4)]
            for zl in range(2)
        ]
    )
    angle = order.astype(np.float32)[..., None] * freq.astype(np.float32)
    cosine, sine = np.cos(angle.astype(np.float64)), np.sin(angle.astype(np.float64))
    both = np.stack(
        [np.concatenate([cosine, cosine], -1), np.concatenate([-sine, sine], -1)], axis=1
    )
    return both.astype(np.float32)


def fold_view(ref, me, lead, axis, row, rows, cut):
    head = (ALL,) * lead

    def view(slot, part):
        start, size = row, rows
        if part == 0:
            size = cut
        if part == 1:
            start, size = row + cut, rows - cut
        if axis == "y":
            where = (ALL, slot, ALL)
        else:
            where = (lax.rem(slot, 2), ALL, lax.div(slot, 2))
        return ref.at[head + where + (pl.ds(start, size), ALL)]

    return view


def kernel_feed(
    h_in, cot_in, mlp_in, y_in, gains_in,
    part_out, dattn_out, fold_y_out, fold_z_out, dy_out, gain_out,
    w_mlp, h_two, cot, gate_s, up_s, act_s, d_gate, d_up, act, flipped, flipped_far,
    h_far, cot_far, part, near_left, near_right, whole_left, whole_right, d_attn, out_part,
    *rest,
):
    bufs, (send, recv, local) = list(rest[:-3]), rest[-3:]
    bufs = [tuple(bufs[4 * i : 4 * i + 4]) for i in range(len(bufs) // 4)]
    me = place()
    wire = Wire(send, recv, local)
    loads = [
        wire.move(h_in, h_two),
        wire.move(mlp_in.at[0], w_mlp.at[0]),
        wire.move(mlp_in.at[1], w_mlp.at[1]),
        wire.move(cot_in, cot),
        wire.move(mlp_in.at[2], w_mlp.at[2]),
    ]
    greet(me, False)

    def whole(which, zl):
        return jnp.concatenate(
            [
                w_mlp[which, zl, y, zh, core]
                for y in range(4)
                for zh in range(2)
                for core in range(2)
            ],
            axis=1,
        )

    def share(source, target):
        return [
            wire.put(
                source.at[:, :, pl.ds(pl.multiple_of((block * 2 + 1 - me.core) * 128, 128), 128)],
                target.at[block],
                sibling(me),
            )
            for block in range(8)
        ]

    loads[0].wait()
    h_puts = share(h_two, h_far)
    loads[1].wait()
    gate_s[...] = dot_nt(h_two[...].reshape(512, D), whole(0, 0))
    loads[2].wait()
    up_s[...] = dot_nt(h_two[...].reshape(512, D), whole(1, 0))
    loads[3].wait()
    cot_puts = share(cot, cot_far)
    loads[4].wait()
    far = []

    def forward(zl):
        act_s[...] = dot_nt(cot[...].reshape(512, D), whole(2, zl))

        def inner(index, carry):
            span = pl.ds(pl.multiple_of(index * 32, 32), 32)
            gate, up, d_act = gate_s[span, :], up_s[span, :], act_s[span, :]
            sigma = 1.0 / (1.0 + jnp.exp(-gate))
            act[zl, span, :] = (gate * sigma * up).astype(BF)
            d_gate[zl, span, :] = (d_act * up * sigma * (1.0 + gate * (1.0 - sigma))).astype(BF)
            d_up[zl, span, :] = (d_act * gate * sigma).astype(BF)
            return carry

        lax.fori_loop(0, 16, inner, 0)

    forward(0)
    gate_s[...] = dot_nt(h_two[...].reshape(512, D), whole(0, 1))
    up_s[...] = dot_nt(h_two[...].reshape(512, D), whole(1, 1))
    forward(1)

    def back_h(block, carry):
        y, zh = lax.div(block, 2), lax.rem(block, 2)
        total = None
        for which, left in ((0, d_gate), (1, d_up)):
            for zl in range(2):
                weight = jnp.concatenate(
                    [w_mlp[which, zl, y, zh, 0], w_mlp[which, zl, y, zh, 1]], axis=1
                )
                term = dot_nn(left[zl], weight)
                total = term if total is None else total + term
        part[:, :, pl.ds(pl.multiple_of(block * 256, 256), 256)] = total.astype(BF).reshape(4, 128, 256)
        return carry

    total = RingSum(
        wire, me, "x", columns_of(part), near_left, near_right, whole_left, whole_right,
        split_columns, lambda target, term: add_into(target, [term]),
    )
    lax.fori_loop(0, 4, back_h, 0)
    total.start((0,))
    lax.fori_loop(4, 8, back_h, 0)
    total.start((1,))

    for which, source in enumerate((d_gate, d_up, act)):
        for zl in range(2):
            flipped[which, zl] = source[zl].T
        far.append(wire.put(flipped.at[which], flipped_far.at[which], sibling(me)))

    def forward_down(block, carry):
        y, zh = lax.div(block, 2), lax.rem(block, 2)
        result = None
        for zl in range(2):
            weight = jnp.concatenate([w_mlp[2, zl, y, zh, 0], w_mlp[2, zl, y, zh, 1]], axis=1)
            term = dot_nn(act[zl], weight)
            result = term if result is None else result + term
        out_part[:, :, pl.ds(pl.multiple_of(block * 256, 256), 256)] = result.astype(BF).reshape(4, 128, 256)
        return carry

    lax.fori_loop(0, 8, forward_down, 0)
    kept = [wire.move(out_part, part_out)]
    total.relay()

    def grad(which, rows, rows_far):
        def body(index, carry):
            zl, y = lax.div(index, 4), lax.rem(index, 4)
            mine = jnp.concatenate(
                [
                    rows[:, :, pl.ds(pl.multiple_of(((y * 2 + zh) * 2 + me.core) * 128, 128), 128)]
                    .reshape(512, 128)
                    for zh in range(2)
                ],
                axis=1,
            )
            other = jnp.concatenate(
                [rows_far[y * 2 + zh].reshape(512, 128) for zh in range(2)], axis=1
            )
            result = dot_nn(flipped[which, zl], mine) + dot_nn(flipped_far[which, zl], other)
            result = result.astype(BF)
            w_mlp[which, zl, y, 0, 0] = result[:, 0:128]
            w_mlp[which, zl, y, 1, 0] = result[:, 128:256]
            return carry

        return body

    def add(target, term):
        add_into(target, [term])

    sums = []

    def start_sums(which):
        ref = w_mlp.at[which, :, :, :, 0]
        pair = [
            RingSum(wire, me, "y", fold_view(ref, me, 0, "y", 0, 352, 176), *bufs[2 * which],
                    split_rows(176), add),
            RingSum(wire, me, "z", fold_view(ref, me, 0, "z", 352, 336, 176), *bufs[2 * which + 1],
                    split_rows(176), add),
        ]
        for item in pair:
            item.start()
        sums.append(pair)

    for copy in h_puts:
        copy.wait_recv()
    far[0].wait_recv()
    lax.fori_loop(0, 8, grad(0, h_two, h_far), 0)
    start_sums(0)
    far[1].wait_recv()
    lax.fori_loop(0, 8, grad(1, h_two, h_far), 0)
    start_sums(1)
    total.finish()

    gain_two = gains_in[1:2, :]

    def back_norm(index, carry):
        span = pl.ds(pl.multiple_of(index * 16, 16), 16)
        d_h = (
            part[me.x, span, :].astype(F32)
            + whole_left[span, :].astype(F32)
            + whole_right[span, :].astype(F32)
        )
        value = y_in[span, :]
        scale = lax.rsqrt(jnp.mean(value * value, axis=-1, keepdims=True) + EPS)
        normed = value * scale
        e_two = d_h * gain_two
        inner = jnp.mean(e_two * normed, axis=-1, keepdims=True)
        d_y = cot[me.x, span, :].astype(F32) + scale * (e_two - normed * inner)
        dy_out[span, :] = d_y
        d_attn[me.x, span, :] = d_y.astype(BF)
        return carry + jnp.sum(d_h * normed, axis=0, keepdims=True)

    gain_out[...] = lax.fori_loop(0, 8, back_norm, jnp.zeros((1, D), F32))
    d_ring = Ring(wire, me, "x", rows_of(d_attn)).start()
    far[2].wait_recv()
    for copy in cot_puts:
        copy.wait_recv()
    lax.fori_loop(0, 8, grad(2, cot, cot_far), 0)
    start_sums(2)
    for item in sums[0] + sums[1]:
        item.relay()
    d_ring.relay()
    for item in sums[2]:
        item.relay()
    for which, pair in enumerate(sums):
        for item, out in zip(pair, (fold_y_out, fold_z_out)):
            item.finish()
            mine = item.part(item.at, None)
            add_into(mine, list(item.whole))
            kept.append(wire.move(mine, out.at[which]))
    d_ring.close().finish()
    kept.append(wire.move(d_attn, dattn_out))
    for copy in kept:
        copy.wait()
    wire.drain()


def fold_shapes(lead, count, rows, cut, columns):
    return [
        pltpu.VMEM((*lead, *count, cut, columns), BF),
        pltpu.VMEM((*lead, *count, rows - cut, columns), BF),
        pltpu.VMEM((*lead, *count, rows, columns), BF),
        pltpu.VMEM((*lead, *count, rows, columns), BF),
    ]


def call_feed(h_two, cot, mlp, y_one, gains):
    shape = jax.ShapeDtypeStruct
    bufs = (fold_shapes((), (2, 2), 352, 176, 128) + fold_shapes((), (4,), 336, 176, 128)) * 3
    return pl.pallas_call(
        kernel_feed,
        name="feed",
        in_specs=[anywhere()] * 3 + [in_vmem()] * 2,
        out_specs=[anywhere()] * 4 + [in_vmem()] * 2,
        out_shape=[
            shape((4, 128, D), BF),
            shape((4, 128, D), BF),
            shape((3, 2, 2, 352, 128), BF),
            shape((3, 4, 336, 128), BF),
            shape((128, D), F32),
            shape((1, D), F32),
        ],
        scratch_shapes=[
            pltpu.VMEM((3, 2, 4, 2, 2, UNITS, 128), BF),
            pltpu.VMEM((4, 128, D), BF),
            pltpu.VMEM((4, 128, D), BF),
            pltpu.VMEM((512, UNITS), F32),
            pltpu.VMEM((512, UNITS), F32),
            pltpu.VMEM((512, UNITS), F32),
            pltpu.VMEM((2, 512, UNITS), BF),
            pltpu.VMEM((2, 512, UNITS), BF),
            pltpu.VMEM((2, 512, UNITS), BF),
            pltpu.VMEM((3, 2, UNITS, 512), BF),
            pltpu.VMEM((3, 2, UNITS, 512), BF),
            pltpu.VMEM((8, 4, 128, 128), BF),
            pltpu.VMEM((8, 4, 128, 128), BF),
            pltpu.VMEM((4, 128, D), BF),
            pltpu.VMEM((128, D // 2), BF),
            pltpu.VMEM((128, D // 2), BF),
            pltpu.VMEM((128, D), BF),
            pltpu.VMEM((128, D), BF),
            pltpu.VMEM((4, 128, D), BF),
            pltpu.VMEM((4, 128, D), BF),
        ]
        + bufs
        + [
            pltpu.SemaphoreType.DMA((100,)),
            pltpu.SemaphoreType.DMA((100,)),
            pltpu.SemaphoreType.DMA((24,)),
        ],
        compiler_params=pltpu.CompilerParams(
            collective_id=1, has_side_effects=True, vmem_limit_bytes=VMEM_BYTES
        ),
    )(h_two, cot, mlp, y_one, gains)


class Fold:
    def __init__(self, wire, me, cut, view_one, axes, bufs, view_two, bufs_two):
        def add(target, term):
            add_into(target, [term])

        self.wire, self.me, self.axes, self.add = wire, me, axes, add
        self.view_two, self.bufs_two = view_two, bufs_two
        self.one, self.split = None, split_rows(cut)
        if view_one is not None:
            self.one = RingSum(wire, me, axes[0], view_one, *bufs, self.split, add)

    def start(self):
        self.one.start()

    def relay(self):
        self.one.relay()

    def turn(self):
        if self.one is not None:
            self.one.finish()
            add_into(self.one.part(self.one.at, None), list(self.one.whole))
        self.two = RingSum(self.wire, self.me, self.axes[1], self.view_two, *self.bufs_two, self.split, self.add)
        self.two.start()

    def relay_two(self):
        self.two.relay()

    def finish(self, result):
        self.two.finish()
        add_into(self.two.part(self.two.at, None), list(self.two.whole), result)


def crossed_view(ref, me, lead, axis, row, rows, cut):
    head = (ALL,) * lead

    def view(slot, part):
        start, size = row, rows
        if part == 0:
            size = cut
        if part == 1:
            start, size = row + cut, rows - cut
        if axis == "z":
            where = (lax.rem(slot, 2), me.y, lax.div(slot, 2))
        else:
            where = (me.zl, slot, me.zh)
        return ref.at[head + where + (pl.ds(start, size), ALL)]

    return view


def held_view(ref, lead, axis, rows, cut):
    head = (ALL,) * lead

    def view(slot, part):
        start, size = 0, rows
        if part == 0:
            size = cut
        if part == 1:
            start, size = cut, rows - cut
        where = (lax.rem(slot, 2), lax.div(slot, 2)) if axis == "z" else (slot,)
        return ref.at[head + where + (pl.ds(start, size), ALL)]

    return view


def kernel_back(
    start_in, tokens_in, dattn_in, part_in, qkv_in, wo_in, query_in, keys_in, values_in, heads_in,
    lse_in, turned_in, tables_in, gains_in, y_in, dy_in, gain_in, fold_y_in, fold_z_in,
    result_out, tokens_out, g_qkv_out, g_o_out, g_mlp_out, gains_out,
    w_qkv, w_o, d_attn, out_part, tables, bias, tok, turned, d_heads, d_query, d_keys, d_values,
    d_query_far, d_keys_far, d_values_far, sum_keys, sum_values, heads_t, heads_t_far, attn_far,
    d_h, far_one, side_left, side_right, last_z,
    near_left, near_right, whole_left, whole_right,
    out_near_left, out_near_right, out_whole_left, out_whole_right,
    g_qkv, g_o, fold_y, fold_z, gain_t, gain_x, gain_z, gain_c,
    *rest,
):
    bufs, (send, recv, local) = list(rest[:-3]), rest[-3:]
    bufs = [tuple(bufs[4 * i : 4 * i + 4]) for i in range(len(bufs) // 4)]
    me = place()
    wire = Wire(send, recv, local)
    greet(me, True)
    loads = [
        wire.move(dattn_in, d_attn),
        wire.move(wo_in, w_o),
        wire.move(fold_y_in, fold_y),
        wire.move(fold_z_in, fold_z),
        wire.move(part_in, out_part),
        wire.move(tables_in.at[me.zl], tables),
        wire.move(qkv_in, w_qkv),
        wire.move(tokens_in, tok),
        wire.move(turned_in, turned),
    ]
    for copy in loads[2:4]:
        copy.wait()
    feed = [
        Fold(wire, me, 176, None, ("y", "z"), None, held_view(fold_y, 1, "z", 352, 176), bufs[0]),
        Fold(wire, me, 176, None, ("z", "y"), None, held_view(fold_z, 1, "y", 336, 176), bufs[1]),
    ]
    for item in feed:
        item.turn()
    loads[0].wait()
    attn_puts = []
    for block in range(8):
        column = pl.ds(pl.multiple_of((block * 2 + 1 - me.core) * 128, 128), 128)
        attn_puts.append(wire.put(d_attn.at[:, :, column], attn_far.at[block], sibling(me)))
    heads_t[...] = heads_in[...].T
    heads_put = wire.put(heads_t, heads_t_far, sibling(me))
    loads[4].wait()

    def add(target, term):
        add_into(target, [term])

    total = RingSum(
        wire, me, "x", columns_of(out_part), out_near_left, out_near_right, out_whole_left,
        out_whole_right, split_columns, add,
    ).start()
    loads[1].wait()

    def back_heads(zl, carry):
        weight = jnp.concatenate(
            [w_o[zl, y, zh, c] for y in range(4) for zh in range(2) for c in range(2)], axis=1
        )
        result = dot_nt(d_attn[...].reshape(512, D), weight).astype(BF)
        d_heads[zl * 2] = result[:, 0:HD]
        d_heads[zl * 2 + 1] = result[:, HD : 2 * HD]
        return carry

    lax.fori_loop(0, 2, back_heads, 0)
    fill_bias(bias, me, start_in[0])
    loads[5].wait()

    def grad_o(index, carry):
        zl, y = lax.div(index, 4), lax.rem(index, 4)
        mine = jnp.concatenate(
            [
                d_attn[:, :, pl.ds(pl.multiple_of(((y * 2 + zh) * 2 + me.core) * 128, 128), 128)]
                .reshape(512, 128)
                for zh in range(2)
            ],
            axis=1,
        )
        other = jnp.concatenate(
            [attn_far[y * 2 + zh].reshape(512, 128) for zh in range(2)], axis=1
        )
        rows = pl.ds(pl.multiple_of(zl * 256, 256), 256)
        result = (dot_nn(heads_t[rows, :], mine) + dot_nn(heads_t_far[rows, :], other)).astype(BF)
        g_o[zl, y, 0] = result[:, 0:128]
        g_o[zl, y, 1] = result[:, 128:256]
        return carry

    heads_put.wait_recv()
    for copy in attn_puts:
        copy.wait_recv()
    lax.fori_loop(0, 8, grad_o, 0)
    attn = [
        Fold(wire, me, 64, fold_view(g_o, me, 0, "y", 0, 128, 64), ("y", "z"), bufs[2],
             crossed_view(g_o, me, 0, "z", 0, 128, 64), bufs[3]),
        Fold(wire, me, 64, fold_view(g_o, me, 0, "z", 128, 128, 64), ("z", "y"), bufs[4],
             crossed_view(g_o, me, 0, "y", 128, 128, 64), bufs[5]),
    ]
    for item in attn:
        item.start()
    total.relay()
    for item in feed:
        item.relay_two()

    def back_attend(head, carry):
        for half, pairs in ((1, 4), (0, 3)):
            span = pairs * 256
            rows = slice(half * 256, half * 256 + 256)
            key = keys_in[head, 0:pairs].reshape(span, HD)
            value = values_in[head, 0:pairs].reshape(span, HD)
            query, d_head = query_in[head, rows, :], d_heads[head, rows, :]
            scores = dot_nt(key, query) * SCALE + bias[0:span, rows]
            probs = jnp.exp(scores - lse_in[head, :, rows])
            d_probs = dot_nt(value, d_head)
            delta = jnp.sum(probs * d_probs, axis=0, keepdims=True)
            d_scores = (probs * (d_probs - delta) * SCALE).astype(BF)
            d_key = dot_nn(d_scores, query)
            d_value = dot_nn(probs.astype(BF), d_head)
            if half == 1:
                sum_keys[...] = d_key
                sum_values[...] = d_value
            else:
                sum_keys[0:span, :] += d_key
                sum_values[0:span, :] += d_value
            raw = dot_tn(key, d_scores).T
            cosine = tables[0, 2 * half : 2 * half + 2, 0].reshape(256, HD)
            sine = tables[1, 2 * half : 2 * half + 2, 0].reshape(256, HD)
            column = pl.ds(pl.multiple_of(head * HD, HD), HD)
            d_query[rows, column] = turn(raw, cosine, -sine).astype(BF)
        cosine, sine = tables[0].reshape(SEQ, HD), tables[1].reshape(SEQ, HD)
        d_keys[:, column] = turn(sum_keys[...], cosine, -sine).astype(BF)
        d_values[:, column] = sum_values[...].astype(BF)
        return carry

    lax.fori_loop(0, 2, back_attend, 0)
    for item in attn:
        item.relay()
    for item, out in zip(feed, (g_mlp_out.at[:, 0:352, :], g_mlp_out.at[:, 352:UNITS, :])):
        item.finish(out)
    lax.fori_loop(2, 4, back_attend, 0)
    grads_put = [
        wire.put(d_query, d_query_far, sibling(me)),
        wire.put(d_keys, d_keys_far, sibling(me)),
        wire.put(d_values, d_values_far, sibling(me)),
    ]
    for item in attn:
        item.turn()
    for copy in loads[6:]:
        copy.wait()

    def back_h(block, carry):
        y, zh = lax.div(block, 2), lax.rem(block, 2)

        def weight(which):
            return jnp.concatenate(
                [w_qkv[which, 0, y, zh].reshape(256, 256), w_qkv[which, 1, y, zh].reshape(256, 256)],
                axis=1,
            )

        column = pl.ds(pl.multiple_of(block * 256, 256), 256)
        both = dot_nt(d_keys[...], weight(1)) + dot_nt(d_values[...], weight(2))
        both = both.reshape(4, 2, 128, 256)
        own = dot_nt(d_query[...], weight(0)).reshape(4, 128, 256) + both[:, 0]
        d_h[:, 0, :, column] = own.astype(BF)
        d_h[:, 1, :, column] = both[:, 1].astype(BF)
        return carry

    lax.fori_loop(0, 8, back_h, 0)
    one, far, three = rem4(me.x + 1), rem4(me.x + 2), rem4(me.x + 3)
    to_z = wire.put(d_h.at[far, 1], far_one, partner(me))
    to_right = wire.put(d_h.at[one, 1], side_left, near(me, "x", 1))
    to_left = wire.put(d_h.at[three, 1], side_right, near(me, "x", 3))

    total.finish()

    def finish_out(index, carry):
        span = pl.ds(pl.multiple_of(index * 16, 16), 16)
        result_out[span, :] = (
            y_in[span, :]
            + (
                out_part[me.x, span, :].astype(F32)
                + out_whole_left[span, :].astype(F32)
                + out_whole_right[span, :].astype(F32)
            )
        ).astype(BF)
        return carry

    lax.fori_loop(0, 8, finish_out, 0)
    for copy in grads_put:
        copy.wait_recv()

    def blocks(which, pair):
        return turned[which, pl.ds(pair * 4, 4)].reshape(512, SEQ)

    def own_rows(value):
        return jnp.concatenate([value[:, i * 256 : i * 256 + 128] for i in range(4)], axis=1)

    def grad_qkv(index, carry):
        zl, pair = lax.div(index, 2), lax.rem(index, 2)
        column = pl.ds(pl.multiple_of(zl * 256, 256), 256)
        mine, other = blocks(0, pair), blocks(1, pair)
        result = dot_nn(own_rows(mine), d_query[:, column])
        result = result + dot_nn(own_rows(other), d_query_far[:, column])
        g_qkv[0, zl, pl.ds(pair * 2, 2)] = result.astype(BF).reshape(2, 2, 128, 256)
        result = dot_nn(mine, d_keys[:, column]) + dot_nn(other, d_keys_far[:, column])
        g_qkv[1, zl, pl.ds(pair * 2, 2)] = result.astype(BF).reshape(2, 2, 128, 256)
        result = dot_nn(mine, d_values[:, column]) + dot_nn(other, d_values_far[:, column])
        g_qkv[2, zl, pl.ds(pair * 2, 2)] = result.astype(BF).reshape(2, 2, 128, 256)
        return carry

    lax.fori_loop(0, 4, grad_qkv, 0)
    more = [
        Fold(wire, me, 32, fold_view(g_qkv, me, 1, "y", 0, 64, 32), ("y", "z"), bufs[6],
             crossed_view(g_qkv, me, 1, "z", 0, 64, 32), bufs[7]),
        Fold(wire, me, 32, fold_view(g_qkv, me, 1, "z", 64, 64, 32), ("z", "y"), bufs[8],
             crossed_view(g_qkv, me, 1, "y", 64, 64, 32), bufs[9]),
    ]
    for item in more:
        item.start()

    to_z.wait_recv()
    add_into(d_h.at[far, 0], [far_one])
    own_part = RingSum(
        wire, me, "x",
        lambda slot, half: d_h.at[slot, 0] if half is None else d_h.at[slot, 0, :, pl.ds(half * 1024, 1024)],
        near_left, near_right, whole_left, whole_right, split_columns, add,
    ).start()
    to_right.wait_recv()
    to_left.wait_recv()
    add_into(d_h.at[me.x, 1], [side_left, side_right])
    to_z = wire.put(d_h.at[me.x, 1], last_z, partner(me))
    for item in attn:
        item.relay_two()
    own_part.relay()
    for item in more:
        item.relay()
    for item, out in zip(attn, (g_o_out.at[0:128, :], g_o_out.at[128:256, :])):
        item.finish(out)
    for item in more:
        item.turn()
    own_part.finish()
    to_z.wait_recv()

    gain_one = gains_in[0:1, :]

    def back_norm(index, carry):
        span = pl.ds(pl.multiple_of(index * 16, 16), 16)
        d_h_one = (
            d_h[me.x, 0, span, :].astype(F32)
            + whole_left[span, :].astype(F32)
            + whole_right[span, :].astype(F32)
            + last_z[span, :].astype(F32)
        )
        value = tok[span, :].astype(F32)
        scale = lax.rsqrt(jnp.mean(value * value, axis=-1, keepdims=True) + EPS)
        normed = value * scale
        e_one = d_h_one * gain_one
        inner = jnp.mean(e_one * normed, axis=-1, keepdims=True)
        tokens_out[span, :] = (dy_in[span, :] + scale * (e_one - normed * inner)).astype(BF)
        return carry + jnp.sum(d_h_one * normed, axis=0, keepdims=True)

    gain_t[0:1, :] = lax.fori_loop(0, 8, back_norm, jnp.zeros((1, D), F32))
    gain_t[1:2, :] = gain_in[...]
    for row in range(2):
        for block in range(16):
            gain_x[me.x, row * 16 + block : row * 16 + block + 1, :] = gain_t[
                row : row + 1, block * 128 : block * 128 + 128
            ]
    meet = Meet(wire, me, "x", gain_x)
    for item in more:
        item.relay_two()
    meet.finish()
    gain_z[me.z] = gain_x[0] + gain_x[1] + gain_x[2] + gain_x[3]
    Meet(wire, me, "z", gain_z).finish()
    gain_c[me.core, me.y] = gain_z[0] + gain_z[1] + gain_z[2] + gain_z[3]
    MeetCores(wire, me, gain_c).finish()
    total = gain_c[0, 0]
    for core, y in ((0, 1), (0, 2), (0, 3), (1, 0), (1, 1), (1, 2), (1, 3)):
        total = total + gain_c[core, y]
    gains_out[...] = total
    for item, out in zip(more, (g_qkv_out.at[:, 0:64, :], g_qkv_out.at[:, 64:128, :])):
        item.finish(out)
    wire.drain()


def call_back(starts, tokens, d_attn, out_part, qkv, w_out, query, keys, values, heads, lse, turned,
              tables, gains, y_one, d_y, gain_two, fold_y, fold_z):
    shape = jax.ShapeDtypeStruct
    bufs = (
        fold_shapes((3,), (), 352, 176, 128)
        + fold_shapes((3,), (), 336, 176, 128)
        + fold_shapes((), (2, 2), 128, 64, 128)
        + fold_shapes((), (), 128, 64, 128)
        + fold_shapes((), (4,), 128, 64, 128)
        + fold_shapes((), (), 128, 64, 128)
        + fold_shapes((3,), (2, 2), 64, 32, 256)
        + fold_shapes((3,), (), 64, 32, 256)
        + fold_shapes((3,), (4,), 64, 32, 256)
        + fold_shapes((3,), (), 64, 32, 256)
    )
    return pl.pallas_call(
        kernel_back,
        name="back",
        in_specs=[pl.BlockSpec(memory_space=pltpu.SMEM)]
        + [anywhere()] * 5
        + [in_vmem()] * 5
        + [anywhere()] * 2
        + [in_vmem()] * 4
        + [anywhere()] * 2,
        out_specs=[in_vmem()] * 6,
        out_shape=[
            shape((128, D), BF),
            shape((128, D), BF),
            shape((3, 128, 256), F32),
            shape((256, 128), F32),
            shape((3, UNITS, 128), F32),
            shape((32, 128), F32),
        ],
        scratch_shapes=[
            pltpu.VMEM((3, 2, 4, 2, 2, 128, 256), BF),
            pltpu.VMEM((2, 4, 2, 2, 256, 128), BF),
            pltpu.VMEM((4, 128, D), BF),
            pltpu.VMEM((4, 128, D), BF),
            pltpu.VMEM((2, 4, 2, 128, HD), F32),
            pltpu.VMEM((SEQ, 512), F32),
            pltpu.VMEM((128, D), BF),
            pltpu.VMEM((2, 8, 128, SEQ), BF),
            pltpu.VMEM((4, 512, HD), BF),
            pltpu.VMEM((512, 512), BF),
            pltpu.VMEM((SEQ, 512), BF),
            pltpu.VMEM((SEQ, 512), BF),
            pltpu.VMEM((512, 512), BF),
            pltpu.VMEM((SEQ, 512), BF),
            pltpu.VMEM((SEQ, 512), BF),
            pltpu.VMEM((SEQ, HD), F32),
            pltpu.VMEM((SEQ, HD), F32),
            pltpu.VMEM((512, 512), BF),
            pltpu.VMEM((512, 512), BF),
            pltpu.VMEM((8, 4, 128, 128), BF),
            pltpu.VMEM((4, 2, 128, D), BF),
        ]
        + [pltpu.VMEM((128, D), BF)] * 4
        + [
            pltpu.VMEM((128, D // 2), BF),
            pltpu.VMEM((128, D // 2), BF),
            pltpu.VMEM((128, D), BF),
            pltpu.VMEM((128, D), BF),
        ]
        * 2
        + [
            pltpu.VMEM((3, 2, 4, 2, 128, 256), BF),
            pltpu.VMEM((2, 4, 2, 256, 128), BF),
            pltpu.VMEM((3, 2, 2, 352, 128), BF),
            pltpu.VMEM((3, 4, 336, 128), BF),
            pltpu.VMEM((2, D), F32),
            pltpu.VMEM((4, 32, 128), F32),
            pltpu.VMEM((4, 32, 128), F32),
            pltpu.VMEM((2, 4, 32, 128), F32),
        ]
        + bufs
        + [
            pltpu.SemaphoreType.DMA((140,)),
            pltpu.SemaphoreType.DMA((140,)),
            pltpu.SemaphoreType.DMA((16,)),
        ],
        compiler_params=pltpu.CompilerParams(
            collective_id=2, has_side_effects=True, vmem_limit_bytes=VMEM_BYTES
        ),
    )(starts, tokens, d_attn, out_part, qkv, w_out, query, keys, values, heads, lse, turned,
      tables, gains, y_one, d_y, gain_two, fold_y, fold_z)


def kernel_settle(result_in, tokens_in, qkv_in, o_in, mlp_in, gains_in,
                  result, tokens, query, key, value, out, gate, up, down, attn, feed):
    dp, tp = lax.axis_index("dp"), lax.axis_index("tensor")
    result[...] = result_in[...]
    tokens[...] = tokens_in[...]
    for index, target in enumerate((query, key, value)):
        target[...] = qkv_in[index]
    out[...] = o_in[...]
    for index, target in enumerate((gate, up, down)):
        target[...] = mlp_in[index]
    for index, target in enumerate((attn, feed)):
        row = gains_in[pl.ds(index * 16 + dp, 1), :]
        target[...] = pltpu.roll(row, lax.rem(128 - tp * 16, 128), 1)[:, 0:16]


def call_settle(*arrays):
    shape = jax.ShapeDtypeStruct
    return pl.pallas_call(
        kernel_settle,
        name="settle",
        in_specs=[in_vmem()] * 6,
        out_specs=[in_vmem()] * 11,
        out_shape=[shape((128, D), BF)] * 2
        + [shape((128, 256), F32)] * 3
        + [shape((256, 128), F32)]
        + [shape((UNITS, 128), F32)] * 3
        + [shape((1, 16), F32)] * 2,
        compiler_params=pltpu.CompilerParams(vmem_limit_bytes=VMEM_BYTES),
    )(*arrays)


def on_device(tables, tokens, starts, w_query, w_key, w_value, w_out, w_gate, w_up, w_down,
              gain_attn, gain_mlp, cotangent):
    weights = (w_query, w_key, w_value, w_out, w_gate.T, w_up.T, w_down)
    (qkv, w_o, mlp, cot, turned, query, keys, values, heads, h_two, lse, y_one, gains) = call_attend(
        tokens, cotangent, starts, weights, gain_attn.reshape(1, 16), gain_mlp.reshape(1, 16), tables
    )
    out_part, d_attn, fold_y, fold_z, d_y, gain_two = call_feed(h_two, cot, mlp, y_one, gains)
    sums = call_back(
        starts, tokens, d_attn, out_part, qkv, w_o, query, keys, values, heads, lse, turned,
        tables, gains, y_one, d_y, gain_two, fold_y, fold_z,
    )
    result, grad_tokens, query, key, value, out, gate, up, down, attn, feed = call_settle(*sums)
    return (
        result, grad_tokens, query, key, value, out, gate.T, up.T, down,
        attn.reshape(16), feed.reshape(16),
    )


def solution(mesh):
    both = ("dp", "tensor")
    rows, wide, tall = P(both, None), P("dp", "tensor"), P("tensor", "dp")
    in_specs = (
        rows, P("dp"), wide, wide, wide, tall, wide, wide, tall, P(both), P(both), rows,
    )
    out_specs = (
        rows, rows, wide, wide, wide, tall, wide, wide, tall, P(both), P(both),
    )
    return jax.shard_map(
        functools.partial(on_device, rope_tables()), mesh=mesh, in_specs=in_specs,
        out_specs=out_specs, check_vma=False,
    )
```

time: 367 us -> 295 us (0.80)
  Pallas kernels: 352 us -> 293 us
  local copies, waits for them, and re-layouts: 10.5 us -> 0 us
    pallas_call x1, Pallas kernels: 154 us -> 119 us  [call_attend(): pl.pallas_call(kernel_attend, name='attend', in_specs=[anywhere(), anywhe...]
    pallas_call x1 -> x2, Pallas kernels: 99.1 us -> 84 us  [the longest x1 80.8 us: call_feed(): pl.pallas_call(kernel_feed, name='feed', in_specs=[anywhere()] * 3 + [in_...]
    pallas_call x1, Pallas kernels: 98.6 us -> 90.4 us  [call_back(): pl.pallas_call(kernel_back, name='back', in_specs=[pl.BlockSpec(memory_sp...]
    unnamed x20 -> x0, local copies, waits for them, and re-layouts: 6.91 us -> none
where the time goes in v2:
time: 295 us; the launch traced here: 294 us
  Pallas kernels  293 us (99%)
    pallas_call x1, Pallas kernels, call_attend(): pl.pallas_call(kernel_attend, name='attend', in_specs=[anywhere(), anywhe...  119 us
    pallas_call x1, Pallas kernels, call_back(): pl.pallas_call(kernel_back, name='back', in_specs=[pl.BlockSpec(memory_sp...  90.4 us
    pallas_call x1, Pallas kernels, call_feed(): pl.pallas_call(kernel_feed, name='feed', in_specs=[anywhere()] * 3 + [in_...  80.8 us

profile of v2, /device:TPU:1, one launch (start us, length us, event | category | flops | bytes accessed | tf_op | source)
XLA Modules:
  0.0 294.5 jit_solution(1843740701209208533)
XLA Ops:
  1.3 118.7 %attend.1 = (bf16[3,2,4,2,2,128,256]{6,5,4,3,2,1,0:T(8,128)(2,1)}, bf16[2,4,2,2,256,128]{5,4,3,2,1,0:T(8,128)(2,1)}, bf16[3,2,4,2,2,688,128]{6,5,4,3,2,1,0:T(8,1...) custom-call(bf16[128,2048]{1,0:T(8,128)(2,1)} %tokens_in.3, ...), custom_call_target="tpu_custom_call" | custom-call | tf_op jit(solution)/shard_map/attend/pallas_call | solution.py:619
  120.0 80.8 %feed.1 = (bf16[4,128,2048]{2,1,0:T(8,128)(2,1)}, bf16[4,128,2048]{2,1,0:T(8,128)(2,1)}, bf16[3,2,2,352,128]{4,3,2,1,0:T(8,128)(2,1)}, bf16[3,4,336,128]{3,2,1,0...) custom-call(bf16[4,128,2048]{2,1,0:T(8,128)(2,1)} %get-tuple-element.47.h_in, ...), custom_call_target="tpu_custom_call" | custom-call | tf_op jit(solution)/shard_map/feed/pallas_call | solution.py:913
  200.9 90.4 %back.1 = (bf16[128,2048]{1,0:T(8,128)(2,1)}, bf16[128,2048]{1,0:T(8,128)(2,1)}, f32[3,128,256]{2,1,0:T(8,128)}, f32[256,128]{1,0:T(8,128)}, f32[3,688,128]{2,1,0:T(8,128)}, /*index=5*/f32[32,128]{1,0:T(8,128)}) custom-call(s32[1]{0:T(128)S(6)} %copy.24.start_in, bf16[128,2048]{1,0:T(8,128)(2,1)} %tokens_in.3, ...), custom_call_target="tpu_custom_call" | custom-call | tf_op jit(solution)/shard_map/back/pallas_call | solution.py:1323
  291.3 3.2 %settle.1 = (bf16[128,2048]{1,0:T(8,128)(2,1)}, bf16[128,2048]{1,0:T(8,128)(2,1)}, f32[128,256]{1,0:T(8,128)}, f32[128,256]{1,0:T(8,128)}, f32[128,256]{1,0:T(8,...) custom-call(bf16[128,2048]{1,0:T(8,128)(2,1)} %get-tuple-element.66., ...), custom_call_target="tpu_custom_call" | custom-call | tf_op jit(solution)/shard_map/settle/pallas_call | solution.py:1412
